TPU v7x, 256 devices: a whole 4x4x8 slice. The times are simulated.
256 devices in a mesh: rows: 256 (over y, z, x, core).
Axes of the slice: x: 4, y: 4, z: 8, core: 2. Of those that a mesh axis runs over, the one named last changes fastest.
Arguments:
- features: bfloat16 [131072, 4096], P('rows'), may hold values from -90 to 90
- sketch_matrix: bfloat16 [4096, 320], replicated, may hold values from -8 to 8
Outputs:
- whitened: float32 [131072, 320], P('rows')
All inputs are finite; a program needn't handle non-finite values.
Results may differ from a plain program's by a relative error of at most 0.0015.
The roundings to bfloat16 on the way count: a program that leaves them out, or rounds other values in their place, can miss the bound.
Values may be sent and summed in bfloat16 or wider, within the bound.
No kernel may reach another device: no remote copies, remote signals or barrier semaphores. Data moves between devices by JAX's collectives and lax.ppermute only.
A program may use at most 64 MiB of HBM per device.

v0:
```python
import functools
import math

import jax
import jax.numpy as jnp
from jax import lax
from jax.experimental import pallas as pl
from jax.experimental.pallas import tpu as pltpu
from jax.sharding import PartitionSpec as P

SKETCH = 320
PAD = 384
BLOCK = 64
LANES = 128
WIDTH = 4 * LANES
F32 = jnp.float32
BF16 = jnp.bfloat16

FIRST_AXIS = ("y", "x")
SECOND_AXIS = ("x", "y")
Z_AXIS = ("z", "z")
STREAM_BITS = ((0, 1), (1, 0))


def coordinates(index):
    return {"c": index & 1, "x": (index >> 1) & 3, "z": (index >> 3) & 7, "y": (index >> 6) & 3}


def role_of(place):
    return place["c"] ^ ((place["x"] + place["y"] + place["z"]) & 1)


def gray(value):
    return value ^ (value >> 1)


def gray_of(place, role, axes):
    return jnp.where(role == 0, *(gray(place[axis]) for axis in axes))


def across(block):
    return lax.ppermute(block, "rows", [(i, i ^ 1) for i in range(lax.axis_size("rows"))])


def exchange(block, axes, bits):
    pairs = []
    for i in range(lax.axis_size("rows")):
        place = coordinates(i)
        role = role_of(place)
        wanted = gray(place[axes[role]]) ^ bits
        place[axes[role]] = next(v for v in range(8) if gray(v) == wanted)
        place["c"] ^= role ^ role_of(place)
        there = ((place["y"] * 8 + place["z"]) * 4 + place["x"]) * 2 + place["c"]
        pairs.append((i, there))
    return lax.ppermute(block, "rows", pairs)


def shifted(block, axes, shift):
    pairs = []
    for i in range(lax.axis_size("rows")):
        place = coordinates(i)
        role = role_of(place)
        place[axes[role]] = (place[axes[role]] + shift) % 4
        place["c"] ^= role ^ role_of(place)
        there = ((place["y"] * 8 + place["z"]) * 4 + place["x"]) * 2 + place["c"]
        pairs.append((i, there))
    return lax.ppermute(block, "rows", pairs)


def ring_scatter(blocks, place):
    own = jnp.where(role_of(place) == 0, *(place[axis] for axis in SECOND_AXIS))
    pick = lambda n: lax.dynamic_index_in_dim(blocks, (own + n) & 3, 0, keepdims=False)
    received = [shifted(pick(n), SECOND_AXIS, n) for n in (1, 3, 2)]
    return (pick(0) + received[0]) + (received[1] + received[2])


def ring_gather(block, place):
    own = jnp.where(role_of(place) == 0, *(place[axis] for axis in SECOND_AXIS))
    received = [(n, shifted(block, SECOND_AXIS, -n)) for n in (1, 3, 2)]
    blocks = jnp.zeros((4, *block.shape), F32)
    for n, part in [(0, block)] + received:
        blocks = lax.dynamic_update_index_in_dim(blocks, part, (own + n) & 3, 0)
    return blocks


def halve(block, place, axes, bit):
    low, high = jnp.split(block, 2)
    upper = (gray_of(place, role_of(place), axes) >> bit) & 1
    sent = exchange(jnp.where(upper == 0, high, low), axes, 1 << bit)
    return jnp.where(upper == 0, low, high) + sent


def double(block, place, axes, bit):
    upper = (gray_of(place, role_of(place), axes) >> bit) & 1
    other = exchange(block, axes, 1 << bit)
    return jnp.concatenate([jnp.where(upper == 0, block, other), jnp.where(upper == 0, other, block)])


def inner_sum(block, place):
    block = ring_scatter(block, place)
    block = halve(block, place, Z_AXIS, 0)
    others = [exchange(block, Z_AXIS, bits) for bits in (2, 4, 6)]
    block = (block + others[0]) + (others[1] + others[2])
    return ring_gather(double(block, place, Z_AXIS, 0), place)


def order(place, half, stream):
    role = role_of(place) ^ half
    code = gray_of(place, role, FIRST_AXIS)
    first, second = STREAM_BITS[stream]
    return role, (((code >> first) & 1) << 2) | (((code >> second) & 1) << 1)


def cross_blocks(id_ref, features, sketches, outs):
    place = coordinates(id_ref[0])

    @pl.loop(0, outs[0][1].shape[0] // 2)
    def _(pair):
        for (half, stream, start), out in outs:
            role, mask = order(place, half, stream)
            there = (role << 4) | (stream << 3) | ((start + 2 * pair) ^ mask)
            columns = features[:, pl.ds(pl.multiple_of(there * LANES, 256), 256)]
            both = jnp.dot(sketches[...], columns, preferred_element_type=F32)
            cross = both[:SKETCH] + both[SKETCH:]
            out[2 * pair] = cross[:, :LANES]
            out[2 * pair + 1] = cross[:, LANES:]


def send_kernel(id_ref, features_hbm, matrix_hbm, sketches, send0, send1, features, matrix, total, sems):
    chunks = sems.shape[1]
    width = features.shape[1] // chunks

    def copies(n):
        columns = pl.ds(pl.multiple_of(n * width, width), width)
        return [
            pltpu.make_async_copy(source.at[:, columns], target.at[:, columns], sems.at[m, n])
            for m, (source, target) in enumerate(((matrix_hbm, matrix), (features_hbm, features)))
        ]

    for n in range(chunks):
        for copy in copies(n):
            copy.start()
    total[...] = jnp.zeros_like(total)

    @pl.loop(0, chunks)
    def _(n):
        for copy in copies(n):
            copy.wait()
        columns = pl.ds(pl.multiple_of(n * width, width), width)
        total[...] += dot_nt(matrix[:, columns], features[:, columns])

    high, low = split(total[...], 2)
    sketches[:SKETCH, :] = high
    sketches[SKETCH:, :] = low
    cross_blocks(id_ref, features, sketches, (((1, 0, 0), send0), ((1, 1, 0), send1)))


def keep_kernel(id_ref, features, sketches, low0, high0, low1, high1):
    wanted = ((0, 0, 0), (0, 0, 4), (0, 1, 0), (0, 1, 4))
    cross_blocks(id_ref, features, sketches, tuple(zip(wanted, (low0, high0, low1, high1))))


def call(kernel, operands, outs, scratch=(), flops=0, limit=24, space=pltpu.VMEM):
    vmem = pl.BlockSpec(memory_space=pltpu.VMEM)
    return pl.pallas_call(
        kernel,
        out_shape=[jax.ShapeDtypeStruct(shape, dtype) for shape, dtype in outs],
        in_specs=[pl.BlockSpec(memory_space=pltpu.SMEM)]
        + [pl.BlockSpec(memory_space=space)] * (len(operands) - 1),
        out_specs=[vmem] * len(outs),
        scratch_shapes=scratch,
        compiler_params=pltpu.CompilerParams(vmem_limit_bytes=limit * 1024 * 1024),
        cost_estimate=pl.CostEstimate(flops=flops, bytes_accessed=4 * 1024 * 1024, transcendentals=0),
    )(*operands)


def scatter_stream(stream, low, high, received):
    first, second = STREAM_BITS[stream]
    back = exchange(high + received[4:], FIRST_AXIS, 1 << first)
    block = low + received[:4]
    back_next = exchange(block[2:] + back[2:], FIRST_AXIS, 1 << second)
    return block[:2] + back[:2] + back_next


def split(value, terms):
    parts = []
    for _ in range(terms):
        part = value.astype(BF16)
        parts.append(part)
        value = value - part.astype(F32)
    return parts


def dot_nt(a, b, precision=None):
    return lax.dot_general(
        a, b, (((1,), (1,)), ((), ())), precision=precision, preferred_element_type=F32
    )


def dot(a, b, precision=None):
    return jnp.dot(a, b, precision=precision, preferred_element_type=F32)


def dot_three(a, b):
    a0, a1 = split(a, 2)
    b0, b1 = split(b, 2)
    return dot(a0, b0) + (dot(a0, b1) + dot(a1, b0))


def stacked(rows, terms):
    parts = split(rows, 3)
    return jnp.concatenate([parts[n] for n in terms], axis=0)


def beside(value):
    lane = lax.broadcasted_iota(jnp.int32, value.shape, 1)
    parts = [part.astype(F32) for part in split(value, 3)]
    turned = [pltpu.roll(part, BLOCK, 1) for part in parts[:2]]
    pairs = ((0, 0), (1, 0), (2, 1))
    return jnp.concatenate(
        [jnp.where(lane < BLOCK, parts[m], turned[n]).astype(BF16) for m, n in pairs], axis=1
    )


UNDER = (0, 1, 0, 2, 0, 1)


def factor_blocks(blocks, outs, meanwhile):
    groups = BLOCK // 8
    lane = lax.broadcasted_iota(jnp.int32, (8, LANES), 1)
    sub = lax.broadcasted_iota(jnp.int32, (8, LANES), 0)
    work = []
    for block in blocks:
        rows = []
        for g in range(groups):
            unit = jnp.where(lane - BLOCK == sub + 8 * g, 1.0, 0.0).astype(F32)
            rows.append(jnp.where(lane < BLOCK, block[8 * g : 8 * g + 8], unit))
        work.append(rows)
    for g in range(groups):
        columns = [
            [
                [
                    jnp.broadcast_to(rows[r][:, 8 * g + j : 8 * g + j + 1], (8, LANES))
                    for r in range(g, groups)
                ]
                for j in range(8)
            ]
            for rows in work
        ]
        for k in range(8):
            for rows, cols, out in zip(work, columns, outs):
                pivot = cols[k][0][k : k + 1, :]
                inverse = 1.0 / pivot
                row = rows[g][k : k + 1, :]
                out[8 * g + k : 8 * g + k + 1, :] = row * lax.rsqrt(pivot)
                scaled = row * inverse
                for j in range(k + 1, 8):
                    factor = cols[j][0][k : k + 1, :] * inverse
                    for r in range(groups - g):
                        cols[j][r] = cols[j][r] - cols[k][r] * factor
                for r in range(g, groups):
                    column = cols[k][r - g]
                    if r == g:
                        column = jnp.where(sub > k, column, 0.0)
                    rows[r] = rows[r] - column * scaled
        if meanwhile:
            meanwhile.pop(0)()


def factor_all(mats, outs, upper):
    column = lax.broadcasted_iota(jnp.int32, (BLOCK, PAD), 1)
    row = lax.broadcasted_iota(jnp.int32, (BLOCK, PAD), 0)
    lane = lax.broadcasted_iota(jnp.int32, (BLOCK, LANES), 1)
    line = lax.broadcasted_iota(jnp.int32, (BLOCK, LANES), 0)
    steps = SKETCH // BLOCK
    meanwhile = []

    def update(mat, change, step, first, last):
        rows = slice(first * BLOCK, last * BLOCK)
        keep = lax.broadcasted_iota(jnp.int32, ((last - first) * BLOCK, PAD), 1)
        keep = (keep < step * BLOCK) | (keep >= (step + 1) * BLOCK)
        mat[rows, :] = jnp.where(keep, mat[rows, :], 0.0) - change

    for step in range(steps):
        here = slice(step * BLOCK, (step + 1) * BLOCK)
        window = slice(step // 2 * LANES, (step // 2 + 1) * LANES)
        odd = step % 2 == 1
        blocks = []
        for mat in mats:
            block = mat[here, window]
            blocks.append(pltpu.roll(block, BLOCK, 1) if odd else block)
        factor_blocks(blocks, outs, meanwhile)
        inside = (column >= step * BLOCK) & (column < (step + 1) * BLOCK)
        for n, (mat, out) in enumerate(zip(mats, outs)):
            both = out[...]
            inverse = beside(pltpu.roll(both, BLOCK, 1))
            line_up = jnp.where(inside, jnp.where(column - step * BLOCK == row, 1.0, 0.0), mat[here, :])
            panel = dot(inverse, stacked(line_up, UNDER))
            mat[here, :] = panel
            if n == 0:
                upper[here, :] = jnp.where(column >= (step + 1) * BLOCK, panel, 0.0)
                corner = jnp.where((lane < BLOCK) & (lane >= line), both, 0.0)
                corner = pltpu.roll(corner, BLOCK, 1) if odd else corner
                upper[here, window] = upper[here, window] + corner
            if step == steps - 1:
                continue
            start = (step + 1) * BLOCK // LANES * LANES
            turned = jnp.transpose(panel[:, start:])
            turned = jnp.concatenate([turned, jnp.zeros_like(turned)], axis=1)
            left, right = beside(turned), stacked(panel, UNDER)
            skip = (step + 1) * BLOCK - start
            update(mat, dot(left[skip : skip + BLOCK], right), step, step + 1, step + 2)
            if step < steps - 2:

                def rest(mat=mat, left=left, right=right, step=step, skip=skip):
                    stop = SKETCH - start_of(step)
                    update(mat, dot(left[skip + BLOCK : stop], right), step, step + 2, steps)

                def start_of(step):
                    return (step + 1) * BLOCK // LANES * LANES

                meanwhile.append(rest)


def columns_of(place, half, part, stream):
    role, mask = order(place, half, stream)
    first = (role << 4) | (stream << 3) | ((4 * part) ^ (mask & 4))
    return pl.ds(pl.multiple_of(first * LANES, WIDTH), WIDTH)


def pieces_kernel(member, id_ref, sketch_matrix_t, piece, *refs):
    before, (terms, sums, left, right, cross, mix) = refs[:-6], refs[-6:]
    place = coordinates(id_ref[0])
    _, mask = order(place, member[0], member[2])
    for slot in range(4):
        start = (slot ^ (mask & 2)) * LANES
        cross[:, pl.ds(pl.multiple_of(start, LANES), LANES)] = piece[slot]
    a, b, c = split(cross[...], 3)
    for n, (term, again) in enumerate(((a, a), (b, b), (c, a))):
        left[n * SKETCH : (n + 1) * SKETCH, :] = term
        terms[n * SKETCH : (n + 1) * SKETCH, :] = again
    right[:SKETCH, :] = a
    right[SKETCH:PAD, :] = jnp.zeros((PAD - SKETCH, WIDTH), BF16)
    right[PAD:, :] = sketch_matrix_t[:, columns_of(place, *member)]
    both = dot_nt(left[...], right[...])
    parts = [both[n * SKETCH : (n + 1) * SKETCH] for n in range(3)]
    mix[...] = jnp.zeros_like(mix)
    mix[:SKETCH, :SKETCH] = parts[1][:, :SKETCH] + parts[2][:, :SKETCH]
    mixed = (mix[...] + jnp.transpose(mix[...]))[:SKETCH]
    sums[...] = before[0][...] if before else jnp.zeros_like(sums)
    sums[0, :, :SKETCH] += parts[0][:, PAD:] + (parts[1][:, PAD:] + parts[2][:, PAD:])
    sums[1, :, :SKETCH] += parts[0][:, :SKETCH] + dot_nt(b, b)
    sums[1] += mixed


def factor_kernel(scale, id_ref, own, other, basis_map, inverse_c, gram, coupling, upper, out0, out1, wide):
    for n, ref in enumerate((gram, coupling)):
        ref[...] = jnp.zeros_like(ref)
        ref[:SKETCH, :] = own[n] + other[n]
    upper[...] = jnp.zeros_like(upper)
    factor_all((gram, coupling), (out0, out1), upper)
    row = lax.broadcasted_iota(jnp.int32, (PAD, PAD), 0)
    column = lax.broadcasted_iota(jnp.int32, (PAD, PAD), 1)
    lower = (row < SKETCH) & (column <= row)
    high, low = split(jnp.where(lower, gram[...], 0.0)[:SKETCH, :SKETCH], 2)
    for n, term in enumerate((high, high, low)):
        wide[:, n * SKETCH : (n + 1) * SKETCH] = term.astype(F32)
    basis_map[...] = wide[...].astype(BF16)
    chain = dot_three(jnp.where(lower, coupling[...], 0.0), jnp.transpose(upper[...]))
    gram[...] = dot_three(jnp.transpose(chain), chain) * scale
    inverse_c[...] = gram[:SKETCH, :SKETCH]


def final_kernel(members, id_ref, features, basis_map, inverse_c, *refs):
    terms, (result, coeffs) = refs[:-2], refs[-2:]
    place = coordinates(id_ref[0])
    part = WIDTH // 2

    @pl.loop(0, 2)
    def _(n):
        here = pl.ds(pl.multiple_of(n * part, part), part)
        for term, member in zip(terms, members):
            start = pl.multiple_of(columns_of(place, *member).start + n * part, part)
            coeffs[:, pl.ds(start, part)] = dot(basis_map[...], term[:, here]).astype(BF16)

    @pl.loop(0, 2)
    def _(n):
        rows = pl.ds(pl.multiple_of(n * part, part), part)
        result[:, rows] = dot_three(inverse_c[...], dot_nt(coeffs[...], features[rows, :]))


def body(features, sketch_matrix):
    rows, width = features.shape
    rows_total = rows * lax.axis_size("rows")
    device = lax.axis_index("rows").astype(jnp.int32)[None]
    whole, piece = ((8, SKETCH, LANES), F32), ((4, SKETCH, LANES), F32)
    flops = 2 * rows * width * SKETCH

    sketch_matrix_t = sketch_matrix.T

    sketches, send0, send1 = call(
        send_kernel,
        (device, features, sketch_matrix_t),
        [((2 * SKETCH, rows), BF16), whole, whole],
        scratch=[
            pltpu.VMEM((rows, width), BF16),
            pltpu.VMEM((SKETCH, width), BF16),
            pltpu.VMEM((SKETCH, rows), F32),
            pltpu.SemaphoreType.DMA((2, 4)),
        ],
        flops=2 * flops,
        space=pltpu.HBM,
        limit=50,
    )
    received = across(send0), across(send1)
    low0, high0, low1, high1 = call(
        keep_kernel, (device, features, sketches), [piece] * 4, flops=flops
    )
    block = jnp.concatenate(
        [scatter_stream(0, low0, high0, received[0]), scatter_stream(1, low1, high1, received[1])]
    )
    block = inner_sum(block, coordinates(device[0]))
    streams = []
    for stream, (first, second) in enumerate(STREAM_BITS):
        own = block[2 * stream : 2 * stream + 2]
        own = jnp.concatenate([own, exchange(own, FIRST_AXIS, 1 << second)])
        streams.append((own, exchange(own, FIRST_AXIS, 1 << first)))

    members = [(0, part, stream) for part in range(2) for stream in range(2)]
    terms_shape = ((3 * SKETCH, WIDTH), BF16)
    sums_shape = ((2, SKETCH, PAD), F32)
    terms, sums = [], ()
    for member in members:
        _, part, stream = member
        term, *sums = call(
            functools.partial(pieces_kernel, member),
            (device, sketch_matrix_t, streams[stream][part], *sums),
            [terms_shape, sums_shape],
            scratch=[
                pltpu.VMEM(*terms_shape),
                pltpu.VMEM((PAD + SKETCH, WIDTH), BF16),
                pltpu.VMEM((SKETCH, WIDTH), F32),
                pltpu.VMEM((PAD, PAD), F32),
            ],
        )
        terms.append(term)
    square, corner = pltpu.VMEM((PAD, PAD), F32), pltpu.VMEM((BLOCK, LANES), F32)
    basis_map, inverse_c = call(
        functools.partial(factor_kernel, math.sqrt(rows_total)),
        (device, *sums, across(*sums)),
        [((SKETCH, 3 * SKETCH), BF16), ((SKETCH, SKETCH), F32)],
        scratch=[square] * 3 + [corner] * 2 + [pltpu.VMEM((SKETCH, 3 * SKETCH), F32)],
        flops=14 * flops,
    )
    terms += [across(term) for term in terms]
    members += [(1, part, stream) for _, part, stream in members]
    (result,) = call(
        functools.partial(final_kernel, members),
        (device, features, basis_map, inverse_c, *terms),
        [((SKETCH, rows), F32)],
        scratch=[pltpu.VMEM((SKETCH, width), BF16)],
        flops=4 * flops,
    )
    return result.T


def solution(mesh):
    return jax.shard_map(
        body,
        mesh=mesh,
        in_specs=(P("rows", None), P()),
        out_specs=P("rows", None),
        check_vma=False,
    )
```

profile of v0, /device:TPU:1, one launch (start us, length us, event | category | flops | bytes accessed | tf_op | source)
XLA Modules:
  0.0 123.6 jit_solution(1826857371556973351)
XLA Ops:
  0.0 6.0 %shard_map.28 = (bf16[640,512]{1,0:T(8,128)(2,1)S(1)}, f32[8,320,128]{2,1,0:T(8,128)S(1)}, f32[8,320,128]{2,1,0:T(8,128)S(1)}) custom-call(s32[1]{0:T(128)} %bitcast.id_ref, bf16[512,4096]{1,0:T(8,128)(2,1)} %features.3, bf16[320,4096]{1,0:T(8,128)(2,1)} %bitcast.23), custom_call_target="tpu_custom_call" | custom-call | flops 2684354560 | bytes 4194304 | tf_op jit(solution)/shard_map/pallas_call | solution.py:165
  6.0 3.3 %collective-permute-start.3 = (f32[8,320,128]{2,1,0:T(8,128)S(1)}, f32[8,320,128]{2,1,0:T(8,128)S(1)}, u32[]{:S(2)}, u32[]{:S(2)}) collective-permute-start(f32[8,320,128]{2,1,0:T(8,128)S(1)} %get-tuple-element.27), channel_id=1, source_target_pairs={{0,1},{1,0},{2,3},{3,2},{4,5},{5,4},{6,7},{7,6},{8,9},{9,8},{10,11... | collective-permute-start | bytes 3932168 | tf_op jit(solution)/shard_map/ppermute | solution.py:42
  9.4 1.7 %shard_map.29 = (f32[4,320,128]{2,1,0:T(8,128)S(1)}, f32[4,320,128]{2,1,0:T(8,128)S(1)}, f32[4,320,128]{2,1,0:T(8,128)S(1)}, f32[4,320,128]{2,1,0:T(8,128)S(1)}) custom-call(s32[1]{0:T(128)} %bitcast.id_ref, bf16[512,4096]{1,0:T(8,128)(2,1)S(1)} %copy-done.1, bf16[640,512]{1,0:T(8,128)(2,1)S(1)} %get-tuple-element.22.sketches), custom_call_target="tpu_custom_call" | custom-call | flops 1342177280 | bytes 4194304 | tf_op jit(solution)/shard_map/pallas_call | solution.py:165
  14.1 9.3 %collective-permute-done.4 = f32[4,320,128]{2,1,0:T(8,128)S(1)} collective-permute-done((f32[4,320,128]{2,1,0:T(8,128)S(1)}, f32[4,320,128]{2,1,0:T(8,128)S(1)}, u32[]{:S(2)}, u32[]{:S(2)}) %collective-permute-start.4) | collective-permute-done | bytes 655392 | tf_op jit(solution)/shard_map/ppermute | solution.py:55
  26.1 4.3 %collective-permute-done.5 = f32[2,320,128]{2,1,0:T(8,128)S(1)} collective-permute-done((f32[2,320,128]{2,1,0:T(8,128)S(1)}, f32[2,320,128]{2,1,0:T(8,128)S(1)}, u32[]{:S(2)}, u32[]{:S(2)}) %collective-permute-start.5) | collective-permute-done | bytes 327712 | tf_op jit(solution)/shard_map/ppermute | solution.py:55
  30.5 2.4 %collective-permute-done.2 = f32[2,320,128]{2,1,0:T(8,128)} collective-permute-done((f32[2,320,128]{2,1,0:T(8,128)}, f32[2,320,128]{2,1,0:T(8,128)}, u32[]{:S(2)}, u32[]{:S(2)}) %collective-permute-start.2) | collective-permute-done | bytes 327712 | tf_op jit(solution)/shard_map/ppermute | solution.py:55
  34.0 2.4 %collective-permute-start.8 = (f32[320,128]{1,0:T(8,128)S(1)}, f32[320,128]{1,0:T(8,128)S(1)}, u32[]{:S(2)}, u32[]{:S(2)}) collective-permute-start(f32[320,128]{1,0:T(8,128)S(1)} %get-tuple-element.45), channel_id=1, source_target_pairs={{0,4},{1,129},{2,130},{3,7},{4,0},{5,133},{6,134},{7,3},{8,136},{9... | collective-permute-start | bytes 491528 | tf_op jit(solution)/shard_map/ppermute | solution.py:67
  37.1 2.3 %collective-permute-start.7 = (f32[320,128]{1,0:T(8,128)S(1)}, f32[320,128]{1,0:T(8,128)S(1)}, u32[]{:S(2)}, u32[]{:S(2)}) collective-permute-start(f32[320,128]{1,0:T(8,128)S(1)} %get-tuple-element.47), channel_id=1, source_target_pairs={{0,7},{1,192},{2,195},{3,0},{4,3},{5,196},{6,199},{7,4},{8,201},{9... | collective-permute-start | bytes 491528 | tf_op jit(solution)/shard_map/ppermute | solution.py:67
  40.1 2.5 %collective-permute-done.6 = f32[320,128]{1,0:T(8,128)S(1)} collective-permute-done((f32[320,128]{1,0:T(8,128)S(1)}, f32[320,128]{1,0:T(8,128)S(1)}, u32[]{:S(2)}, u32[]{:S(2)}) %collective-permute-start.6) | collective-permute-done | bytes 163872 | tf_op jit(solution)/shard_map/ppermute | solution.py:67
  42.7 1.7 %collective-permute-start.9 = (f32[160,128]{1,0:T(8,128)S(1)}, f32[160,128]{1,0:T(8,128)S(1)}, u32[]{:S(2)}, u32[]{:S(2)}) collective-permute-start(f32[160,128]{1,0:T(8,128)S(1)} %slice_select_fusion), channel_id=1, source_target_pairs={{0,9},{1,8},{2,11},{3,10},{4,13},{5,12},{6,15},{7,14},{8,1},{9,0},... | collective-permute-start | bytes 245768 | tf_op jit(solution)/shard_map/ppermute | solution.py:55
  44.4 2.9 %collective-permute-done.9 = f32[160,128]{1,0:T(8,128)S(1)} collective-permute-done((f32[160,128]{1,0:T(8,128)S(1)}, f32[160,128]{1,0:T(8,128)S(1)}, u32[]{:S(2)}, u32[]{:S(2)}) %collective-permute-start.9) | collective-permute-done | bytes 81952 | tf_op jit(solution)/shard_map/ppermute | solution.py:55
  47.3 6.7 %collective-permute-start.12 = (f32[160,128]{1,0:T(8,128)S(1)}, f32[160,128]{1,0:T(8,128)S(1)}, u32[]{:S(2)}, u32[]{:S(2)}) collective-permute-start(f32[160,128]{1,0:T(8,128)S(1)} %select_add_fusion), channel_id=1, source_target_pairs={{0,32},{1,33},{2,34},{3,35},{4,36},{5,37},{6,38},{7,39},{8,40},{9,... | collective-permute-start | bytes 245768 | tf_op jit(solution)/shard_map/ppermute | solution.py:55
  54.0 1.8 %collective-permute-start.10 = (f32[160,128]{1,0:T(8,128)S(1)}, f32[160,128]{1,0:T(8,128)S(1)}, u32[]{:S(2)}, u32[]{:S(2)}) collective-permute-start(f32[160,128]{1,0:T(8,128)S(1)} %select_add_fusion), channel_id=1, source_target_pairs={{0,25},{1,24},{2,27},{3,26},{4,29},{5,28},{6,31},{7,30},{8,17},{9,... | collective-permute-start | bytes 245768 | tf_op jit(solution)/shard_map/ppermute | solution.py:55
  56.5 5.5 %collective-permute-done.11 = f32[160,128]{1,0:T(8,128)S(1)} collective-permute-done((f32[160,128]{1,0:T(8,128)S(1)}, f32[160,128]{1,0:T(8,128)S(1)}, u32[]{:S(2)}, u32[]{:S(2)}) %collective-permute-start.11) | collective-permute-done | bytes 81952 | tf_op jit(solution)/shard_map/ppermute | solution.py:55
  63.3 3.3 %collective-permute-done.13 = f32[160,128]{1,0:T(8,128)S(1)} collective-permute-done((f32[160,128]{1,0:T(8,128)S(1)}, f32[160,128]{1,0:T(8,128)S(1)}, u32[]{:S(2)}, u32[]{:S(2)}) %collective-permute-start.13) | collective-permute-done | bytes 81952 | tf_op jit(solution)/shard_map/ppermute | solution.py:55
  66.6 2.1 %collective-permute-start.14 = (f32[320,128]{1,0:T(8,128)S(1)}, f32[320,128]{1,0:T(8,128)S(1)}, u32[]{:S(2)}, u32[]{:S(2)}) collective-permute-start(f32[320,128]{1,0:T(8,128)S(1)} %pad_maximum_fusion.2), channel_id=1, source_target_pairs={{0,7},{1,192},{2,195},{3,0},{4,3},{5,196},{6,199},{7,4},{8,201},{9... | collective-permute-start | bytes 491528 | tf_op jit(solution)/shard_map/ppermute | solution.py:67
  71.5 4.8 %collective-permute-done.15 = f32[320,128]{1,0:T(8,128)S(1)} collective-permute-done((f32[320,128]{1,0:T(8,128)S(1)}, f32[320,128]{1,0:T(8,128)S(1)}, u32[]{:S(2)}, u32[]{:S(2)}) %collective-permute-start.15) | collective-permute-done | bytes 163872 | tf_op jit(solution)/shard_map/ppermute | solution.py:67
  76.4 3.2 %collective-permute-start.19 = (f32[2,320,128]{2,1,0:T(8,128)S(1)}, f32[2,320,128]{2,1,0:T(8,128)S(1)}, u32[]{:S(2)}, u32[]{:S(2)}) collective-permute-start(f32[2,320,128]{2,1,0:T(8,128)S(1)} %get-tuple-element.43), channel_id=1, source_target_pairs={{0,193},{1,6},{2,5},{3,194},{4,197},{5,2},{6,1},{7,198},{8,15},{9,... | collective-permute-start | bytes 983048 | tf_op jit(solution)/shard_map/ppermute | solution.py:55
  79.6 4.8 %collective-permute-done.19 = f32[2,320,128]{2,1,0:T(8,128)S(1)} collective-permute-done((f32[2,320,128]{2,1,0:T(8,128)S(1)}, f32[2,320,128]{2,1,0:T(8,128)S(1)}, u32[]{:S(2)}, u32[]{:S(2)}) %collective-permute-start.19) | collective-permute-done | bytes 327712 | tf_op jit(solution)/shard_map/ppermute | solution.py:55
  84.5 1.6 %collective-permute-done.17 = f32[2,320,128]{2,1,0:T(8,128)S(1)} collective-permute-done((f32[2,320,128]{2,1,0:T(8,128)S(1)}, f32[2,320,128]{2,1,0:T(8,128)S(1)}, u32[]{:S(2)}, u32[]{:S(2)}) %collective-permute-start.17) | collective-permute-done | bytes 327712 | tf_op jit(solution)/shard_map/ppermute | solution.py:55
  86.2 1.5 %collective-permute-start.18 = (f32[4,320,128]{2,1,0:T(8,128)S(1)}, f32[4,320,128]{2,1,0:T(8,128)S(1)}, u32[]{:S(2)}, u32[]{:S(2)}) collective-permute-start(f32[4,320,128]{2,1,0:T(8,128)S(1)} %pad_maximum_fusion.piece), channel_id=1, source_target_pairs={{0,193},{1,6},{2,5},{3,194},{4,197},{5,2},{6,1},{7,198},{8,15},{9,... | collective-permute-start | bytes 1966088 | tf_op jit(solution)/shard_map/ppermute | solution.py:55
  90.3 4.5 %collective-permute-done.20.piece = f32[4,320,128]{2,1,0:T(8,128)S(1)} collective-permute-done((f32[4,320,128]{2,1,0:T(8,128)S(1)}, f32[4,320,128]{2,1,0:T(8,128)S(1)}, u32[]{:S(2)}, u32[]{:S(2)}) %collective-permute-start.20) | collective-permute-done | bytes 655392 | tf_op jit(solution)/shard_map/ppermute | solution.py:55
  101.5 14.4 %shard_map.34 = (bf16[320,960]{1,0:T(8,128)(2,1)S(1)}, f32[320,320]{1,0:T(8,128)S(1)}) custom-call(s32[1]{0:T(128)} %bitcast.id_ref, f32[2,320,384]{2,1,0:T(8,128)S(1)} %get-tuple-element.32.own, f32[2,320,384]{2,1,0:T(8,128)S(1)} %collective-permute-done.21.other), custom_call_target="tpu_custom_call" | custom-call | flops 18790481920 | bytes 4194304 | tf_op jit(solution)/shard_map/pallas_call | solution.py:165
  115.9 7.7 %shard_map.35 = f32[320,512]{1,0:T(8,128)} custom-call(s32[1]{0:T(128)} %bitcast.id_ref, bf16[512,4096]{1,0:T(8,128)(2,1)S(1)} %copy-done.2, bf16[320,960]{1,0:T(8,128)(2,1)S(1)} %get-tuple-element.33.basis_map, f32[320,320]{1,0:T(8,128)S(1)} %get-tuple-element.34.inverse_c, bf16[960,512]{1,0:T(8,128)(2,1)S(1)} %get-tuple-element.35.refs_0_, ...), custom_call_target="tpu_custom_call" | custom-call | flops 5368709120 | bytes 4194304 | tf_op jit(solution)/shard_map/pallas_call | solution.py:165
  (63 shorter events, 22.7 us)
Async XLA Ops:
  6.0 6.0 %collective-permute-start.3 = (f32[8,320,128]{2,1,0:T(8,128)S(1)}, f32[8,320,128]{2,1,0:T(8,128)S(1)}, u32[]{:S(2)}, u32[]{:S(2)}) collective-permute-start(f32[8,320,128]{2,1,0:T(8,128)S(1)} %get-tuple-element.27), channel_id=1, source_target_pairs={{0,1},{1,0},{2,3},{3,2},{4,5},{5,4},{6,7},{7,6},{8,9},{9,8},{10,11... | collective-permute-start | bytes 3932168 | tf_op jit(solution)/shard_map/ppermute | solution.py:42
  12.1 11.3 %collective-permute-start.4 = (f32[4,320,128]{2,1,0:T(8,128)S(1)}, f32[4,320,128]{2,1,0:T(8,128)S(1)}, u32[]{:S(2)}, u32[]{:S(2)}) collective-permute-start(f32[4,320,128]{2,1,0:T(8,128)S(1)} %get-tuple-element.40), channel_id=1, source_target_pairs={{0,193},{1,6},{2,5},{3,194},{4,197},{5,2},{6,1},{7,198},{8,15},{9,... | collective-permute-start | bytes 1966088 | tf_op jit(solution)/shard_map/ppermute | solution.py:55
  14.0 10.1 %collective-permute-start.1 = (f32[4,320,128]{2,1,0:T(8,128)S(1)}, f32[4,320,128]{2,1,0:T(8,128)S(1)}, u32[]{:S(2)}, u32[]{:S(2)}) collective-permute-start(f32[4,320,128]{2,1,0:T(8,128)S(1)} %get-tuple-element.42), channel_id=1, source_target_pairs={{0,65},{1,2},{2,1},{3,66},{4,69},{5,6},{6,5},{7,70},{8,11},{9,72},... | collective-permute-start | bytes 1966088 | tf_op jit(solution)/shard_map/ppermute | solution.py:55
  23.5 7.0 %collective-permute-start.5 = (f32[2,320,128]{2,1,0:T(8,128)S(1)}, f32[2,320,128]{2,1,0:T(8,128)S(1)}, u32[]{:S(2)}, u32[]{:S(2)}) collective-permute-start(f32[2,320,128]{2,1,0:T(8,128)S(1)} %slice_add_fusion.4), channel_id=1, source_target_pairs={{0,65},{1,2},{2,1},{3,66},{4,69},{5,6},{6,5},{7,70},{8,11},{9,72},... | collective-permute-start | bytes 983048 | tf_op jit(solution)/shard_map/ppermute | solution.py:55
  24.8 8.0 %collective-permute-start.2 = (f32[2,320,128]{2,1,0:T(8,128)}, f32[2,320,128]{2,1,0:T(8,128)}, u32[]{:S(2)}, u32[]{:S(2)}) collective-permute-start(f32[2,320,128]{2,1,0:T(8,128)} %slice_add_fusion.6), channel_id=1, source_target_pairs={{0,193},{1,6},{2,5},{3,194},{4,197},{5,2},{6,1},{7,198},{8,15},{9,... | collective-permute-start | bytes 983048 | tf_op jit(solution)/shard_map/ppermute | solution.py:55
  34.0 6.1 %collective-permute-start.8 = (f32[320,128]{1,0:T(8,128)S(1)}, f32[320,128]{1,0:T(8,128)S(1)}, u32[]{:S(2)}, u32[]{:S(2)}) collective-permute-start(f32[320,128]{1,0:T(8,128)S(1)} %get-tuple-element.45), channel_id=1, source_target_pairs={{0,4},{1,129},{2,130},{3,7},{4,0},{5,133},{6,134},{7,3},{8,136},{9... | collective-permute-start | bytes 491528 | tf_op jit(solution)/shard_map/ppermute | solution.py:67
  36.4 6.2 %collective-permute-start.6 = (f32[320,128]{1,0:T(8,128)S(1)}, f32[320,128]{1,0:T(8,128)S(1)}, u32[]{:S(2)}, u32[]{:S(2)}) collective-permute-start(f32[320,128]{1,0:T(8,128)S(1)} %get-tuple-element.46), channel_id=1, source_target_pairs={{0,3},{1,64},{2,67},{3,4},{4,7},{5,68},{6,71},{7,0},{8,73},{9,10},... | collective-permute-start | bytes 491528 | tf_op jit(solution)/shard_map/ppermute | solution.py:67
  37.1 5.6 %collective-permute-start.7 = (f32[320,128]{1,0:T(8,128)S(1)}, f32[320,128]{1,0:T(8,128)S(1)}, u32[]{:S(2)}, u32[]{:S(2)}) collective-permute-start(f32[320,128]{1,0:T(8,128)S(1)} %get-tuple-element.47), channel_id=1, source_target_pairs={{0,7},{1,192},{2,195},{3,0},{4,3},{5,196},{6,199},{7,4},{8,201},{9... | collective-permute-start | bytes 491528 | tf_op jit(solution)/shard_map/ppermute | solution.py:67
  42.7 4.6 %collective-permute-start.9 = (f32[160,128]{1,0:T(8,128)S(1)}, f32[160,128]{1,0:T(8,128)S(1)}, u32[]{:S(2)}, u32[]{:S(2)}) collective-permute-start(f32[160,128]{1,0:T(8,128)S(1)} %slice_select_fusion), channel_id=1, source_target_pairs={{0,9},{1,8},{2,11},{3,10},{4,13},{5,12},{6,15},{7,14},{8,1},{9,0},... | collective-permute-start | bytes 245768 | tf_op jit(solution)/shard_map/ppermute | solution.py:55
  47.3 9.2 %collective-permute-start.12 = (f32[160,128]{1,0:T(8,128)S(1)}, f32[160,128]{1,0:T(8,128)S(1)}, u32[]{:S(2)}, u32[]{:S(2)}) collective-permute-start(f32[160,128]{1,0:T(8,128)S(1)} %select_add_fusion), channel_id=1, source_target_pairs={{0,32},{1,33},{2,34},{3,35},{4,36},{5,37},{6,38},{7,39},{8,40},{9,... | collective-permute-start | bytes 245768 | tf_op jit(solution)/shard_map/ppermute | solution.py:55
  54.0 8.0 %collective-permute-start.11 = (f32[160,128]{1,0:T(8,128)S(1)}, f32[160,128]{1,0:T(8,128)S(1)}, u32[]{:S(2)}, u32[]{:S(2)}) collective-permute-start(f32[160,128]{1,0:T(8,128)S(1)} %select_add_fusion), channel_id=1, source_target_pairs={{0,57},{1,56},{2,59},{3,58},{4,61},{5,60},{6,63},{7,62},{8,49},{9,... | collective-permute-start | bytes 245768 | tf_op jit(solution)/shard_map/ppermute | solution.py:55
  54.0 8.0 %collective-permute-start.10 = (f32[160,128]{1,0:T(8,128)S(1)}, f32[160,128]{1,0:T(8,128)S(1)}, u32[]{:S(2)}, u32[]{:S(2)}) collective-permute-start(f32[160,128]{1,0:T(8,128)S(1)} %select_add_fusion), channel_id=1, source_target_pairs={{0,25},{1,24},{2,27},{3,26},{4,29},{5,28},{6,31},{7,30},{8,17},{9,... | collective-permute-start | bytes 245768 | tf_op jit(solution)/shard_map/ppermute | solution.py:55
  62.0 4.5 %collective-permute-start.13 = (f32[160,128]{1,0:T(8,128)S(1)}, f32[160,128]{1,0:T(8,128)S(1)}, u32[]{:S(2)}, u32[]{:S(2)}) collective-permute-start(f32[160,128]{1,0:T(8,128)S(1)} %add_add_fusion), channel_id=1, source_target_pairs={{0,9},{1,8},{2,11},{3,10},{4,13},{5,12},{6,15},{7,14},{8,1},{9,0},... | collective-permute-start | bytes 245768 | tf_op jit(solution)/shard_map/ppermute | solution.py:55
  66.6 4.8 %collective-permute-start.14 = (f32[320,128]{1,0:T(8,128)S(1)}, f32[320,128]{1,0:T(8,128)S(1)}, u32[]{:S(2)}, u32[]{:S(2)}) collective-permute-start(f32[320,128]{1,0:T(8,128)S(1)} %pad_maximum_fusion.2), channel_id=1, source_target_pairs={{0,7},{1,192},{2,195},{3,0},{4,3},{5,196},{6,199},{7,4},{8,201},{9... | collective-permute-start | bytes 491528 | tf_op jit(solution)/shard_map/ppermute | solution.py:67
  68.8 7.5 %collective-permute-start.15 = (f32[320,128]{1,0:T(8,128)S(1)}, f32[320,128]{1,0:T(8,128)S(1)}, u32[]{:S(2)}, u32[]{:S(2)}) collective-permute-start(f32[320,128]{1,0:T(8,128)S(1)} %pad_maximum_fusion.2), channel_id=1, source_target_pairs={{0,3},{1,64},{2,67},{3,4},{4,7},{5,68},{6,71},{7,0},{8,73},{9,10},... | collective-permute-start | bytes 491528 | tf_op jit(solution)/shard_map/ppermute | solution.py:67
  68.8 7.5 %collective-permute-start.16 = (f32[320,128]{1,0:T(8,128)S(1)}, f32[320,128]{1,0:T(8,128)S(1)}, u32[]{:S(2)}, u32[]{:S(2)}) collective-permute-start(f32[320,128]{1,0:T(8,128)S(1)} %pad_maximum_fusion.2), channel_id=1, source_target_pairs={{0,4},{1,129},{2,130},{3,7},{4,0},{5,133},{6,134},{7,3},{8,136},{9... | collective-permute-start | bytes 491528 | tf_op jit(solution)/shard_map/ppermute | solution.py:67
  76.4 8.0 %collective-permute-start.19 = (f32[2,320,128]{2,1,0:T(8,128)S(1)}, f32[2,320,128]{2,1,0:T(8,128)S(1)}, u32[]{:S(2)}, u32[]{:S(2)}) collective-permute-start(f32[2,320,128]{2,1,0:T(8,128)S(1)} %get-tuple-element.43), channel_id=1, source_target_pairs={{0,193},{1,6},{2,5},{3,194},{4,197},{5,2},{6,1},{7,198},{8,15},{9,... | collective-permute-start | bytes 983048 | tf_op jit(solution)/shard_map/ppermute | solution.py:55
  79.6 6.5 %collective-permute-start.17 = (f32[2,320,128]{2,1,0:T(8,128)S(1)}, f32[2,320,128]{2,1,0:T(8,128)S(1)}, u32[]{:S(2)}, u32[]{:S(2)}) collective-permute-start(f32[2,320,128]{2,1,0:T(8,128)S(1)} %get-tuple-element.44), channel_id=1, source_target_pairs={{0,65},{1,2},{2,1},{3,66},{4,69},{5,6},{6,5},{7,70},{8,11},{9,72},... | collective-permute-start | bytes 983048 | tf_op jit(solution)/shard_map/ppermute | solution.py:55
  84.4 10.4 %collective-permute-start.20 = (f32[4,320,128]{2,1,0:T(8,128)S(1)}, f32[4,320,128]{2,1,0:T(8,128)S(1)}, u32[]{:S(2)}, u32[]{:S(2)}) collective-permute-start(f32[4,320,128]{2,1,0:T(8,128)S(1)} %pad_maximum_fusion.1.piece), channel_id=1, source_target_pairs={{0,65},{1,2},{2,1},{3,66},{4,69},{5,6},{6,5},{7,70},{8,11},{9,72},... | collective-permute-start | bytes 1966088 | tf_op jit(solution)/shard_map/ppermute | solution.py:55
  86.2 11.3 %collective-permute-start.18 = (f32[4,320,128]{2,1,0:T(8,128)S(1)}, f32[4,320,128]{2,1,0:T(8,128)S(1)}, u32[]{:S(2)}, u32[]{:S(2)}) collective-permute-start(f32[4,320,128]{2,1,0:T(8,128)S(1)} %pad_maximum_fusion.piece), channel_id=1, source_target_pairs={{0,193},{1,6},{2,5},{3,194},{4,197},{5,2},{6,1},{7,198},{8,15},{9,... | collective-permute-start | bytes 1966088 | tf_op jit(solution)/shard_map/ppermute | solution.py:55
  99.1 16.8 %collective-permute-start.23 = (bf16[960,512]{1,0:T(8,128)(2,1)S(1)}, bf16[960,512]{1,0:T(8,128)(2,1)S(1)}, u32[]{:S(2)}, u32[]{:S(2)}) collective-permute-start(bf16[960,512]{1,0:T(8,128)(2,1)S(1)} %get-tuple-element.36.refs_1_), channel_id=1, source_target_pairs={{0,1},{1,0},{2,3},{3,2},{4,5},{5,4},{6,7},{7,6},{8,9},{9,8},{10,11... | collective-permute-start | bytes 2949128 | tf_op jit(solution)/shard_map/ppermute | solution.py:42
  99.4 16.5 %collective-permute-start.22 = (bf16[960,512]{1,0:T(8,128)(2,1)S(1)}, bf16[960,512]{1,0:T(8,128)(2,1)S(1)}, u32[]{:S(2)}, u32[]{:S(2)}) collective-permute-start(bf16[960,512]{1,0:T(8,128)(2,1)S(1)} %get-tuple-element.35.refs_0_), channel_id=1, source_target_pairs={{0,1},{1,0},{2,3},{3,2},{4,5},{5,4},{6,7},{7,6},{8,9},{9,8},{10,11... | collective-permute-start | bytes 2949128 | tf_op jit(solution)/shard_map/ppermute | solution.py:42
  99.6 16.3 %collective-permute-start.25 = (bf16[960,512]{1,0:T(8,128)(2,1)S(1)}, bf16[960,512]{1,0:T(8,128)(2,1)S(1)}, u32[]{:S(2)}, u32[]{:S(2)}) collective-permute-start(bf16[960,512]{1,0:T(8,128)(2,1)S(1)} %get-tuple-element.38.refs_3_), channel_id=1, source_target_pairs={{0,1},{1,0},{2,3},{3,2},{4,5},{5,4},{6,7},{7,6},{8,9},{9,8},{10,11... | collective-permute-start | bytes 2949128 | tf_op jit(solution)/shard_map/ppermute | solution.py:42
  99.9 16.0 %collective-permute-start.24 = (bf16[960,512]{1,0:T(8,128)(2,1)S(1)}, bf16[960,512]{1,0:T(8,128)(2,1)S(1)}, u32[]{:S(2)}, u32[]{:S(2)}) collective-permute-start(bf16[960,512]{1,0:T(8,128)(2,1)S(1)} %get-tuple-element.37.refs_2_), channel_id=1, source_target_pairs={{0,1},{1,0},{2,3},{3,2},{4,5},{5,4},{6,7},{7,6},{8,9},{9,8},{10,11... | collective-permute-start | bytes 2949128 | tf_op jit(solution)/shard_map/ppermute | solution.py:42
  (5 other events, 40.6 us)
where the time goes:
time: 124 us
  waiting for transfers between devices  53.3 us (43%)
  Pallas kernels  35.1 us (28%)
  starting transfers between devices  32.3 us (26%)
  other arithmetic  2.47 us (2%)
    ppermute x13, waiting for transfers between devices, exchange(): return lax.ppermute(block, 'rows', pairs)  41 us
    pallas_call x8, Pallas kernels, call(): pl.pallas_call(kernel, out_shape=[jax.ShapeDtypeStruct(shape, dtype) for...  35.1 us
    ppermute x13, starting transfers between devices, exchange(): return lax.ppermute(block, 'rows', pairs)  18.9 us
    ppermute x6, waiting for transfers between devices, shifted(): return lax.ppermute(block, 'rows', pairs)  9.42 us
    ppermute x6, starting transfers between devices, shifted(): return lax.ppermute(block, 'rows', pairs)  8.72 us
    ppermute x7, starting transfers between devices, across(): lax.ppermute(block, 'rows', [(i, i ^ 1) for i in range(lax.axis_size('row...  4.71 us
    ppermute x7, waiting for transfers between devices, across(): lax.ppermute(block, 'rows', [(i, i ^ 1) for i in range(lax.axis_size('row...  2.87 us
  transfers between devices with their start and end apart: 26, of which 19 were waited for; matrix products, arithmetic and copies ran while one was open for 1% of the time, Pallas kernels for 16%

commit v1 on v0

--- a/solution.py
+++ b/solution.py
@@ -383,10 +383,8 @@
             start = pl.multiple_of(columns_of(place, *member).start + n * part, part)
             coeffs[:, pl.ds(start, part)] = dot(basis_map[...], term[:, here]).astype(BF16)
 
-    @pl.loop(0, 2)
-    def _(n):
-        rows = pl.ds(pl.multiple_of(n * part, part), part)
-        result[:, rows] = dot_three(inverse_c[...], dot_nt(coeffs[...], features[rows, :]))
+    projected = dot_nt(coeffs[...], features[...])
+    result[...] = dot_three(inverse_c[...], projected)
 
 
 def body(features, sketch_matrix):

time: 124 us -> 123 us (level)
  no operation moved by 1% of the time
where the time goes in v1:
time: 123 us
  waiting for transfers between devices  53.3 us (43%)
  Pallas kernels  34.1 us (28%)
  starting transfers between devices  32.3 us (26%)
  other arithmetic  2.47 us (2%)
    ppermute x13, waiting for transfers between devices, exchange(): return lax.ppermute(block, 'rows', pairs)  41 us
    pallas_call x8, Pallas kernels, call(): pl.pallas_call(kernel, out_shape=[jax.ShapeDtypeStruct(shape, dtype) for...  34.1 us
    ppermute x13, starting transfers between devices, exchange(): return lax.ppermute(block, 'rows', pairs)  18.9 us
    ppermute x6, waiting for transfers between devices, shifted(): return lax.ppermute(block, 'rows', pairs)  9.42 us
    ppermute x6, starting transfers between devices, shifted(): return lax.ppermute(block, 'rows', pairs)  8.72 us
    ppermute x7, starting transfers between devices, across(): lax.ppermute(block, 'rows', [(i, i ^ 1) for i in range(lax.axis_size('row...  4.71 us
    ppermute x7, waiting for transfers between devices, across(): lax.ppermute(block, 'rows', [(i, i ^ 1) for i in range(lax.axis_size('row...  2.87 us
  transfers between devices with their start and end apart: 26, of which 19 were waited for; matrix products, arithmetic and copies ran while one was open for 1% of the time, Pallas kernels for 16%

profile of v1, /device:TPU:1, one launch (start us, length us, event | category | flops | bytes accessed | tf_op | source)
XLA Modules:
  0.0 122.6 jit_solution(5031818733453732224)
XLA Ops:
  0.0 6.0 %shard_map.28 = (bf16[640,512]{1,0:T(8,128)(2,1)S(1)}, f32[8,320,128]{2,1,0:T(8,128)S(1)}, f32[8,320,128]{2,1,0:T(8,128)S(1)}) custom-call(s32[1]{0:T(128)} %bitcast.id_ref, bf16[512,4096]{1,0:T(8,128)(2,1)} %features.3, bf16[320,4096]{1,0:T(8,128)(2,1)} %bitcast.23), custom_call_target="tpu_custom_call" | custom-call | flops 2684354560 | bytes 4194304 | tf_op jit(solution)/shard_map/pallas_call | solution.py:165
  6.0 3.3 %collective-permute-start.3 = (f32[8,320,128]{2,1,0:T(8,128)S(1)}, f32[8,320,128]{2,1,0:T(8,128)S(1)}, u32[]{:S(2)}, u32[]{:S(2)}) collective-permute-start(f32[8,320,128]{2,1,0:T(8,128)S(1)} %get-tuple-element.27), channel_id=1, source_target_pairs={{0,1},{1,0},{2,3},{3,2},{4,5},{5,4},{6,7},{7,6},{8,9},{9,8},{10,11... | collective-permute-start | bytes 3932168 | tf_op jit(solution)/shard_map/ppermute | solution.py:42
  9.4 1.7 %shard_map.29 = (f32[4,320,128]{2,1,0:T(8,128)S(1)}, f32[4,320,128]{2,1,0:T(8,128)S(1)}, f32[4,320,128]{2,1,0:T(8,128)S(1)}, f32[4,320,128]{2,1,0:T(8,128)S(1)}) custom-call(s32[1]{0:T(128)} %bitcast.id_ref, bf16[512,4096]{1,0:T(8,128)(2,1)S(1)} %copy-done.1, bf16[640,512]{1,0:T(8,128)(2,1)S(1)} %get-tuple-element.22.sketches), custom_call_target="tpu_custom_call" | custom-call | flops 1342177280 | bytes 4194304 | tf_op jit(solution)/shard_map/pallas_call | solution.py:165
  14.1 9.3 %collective-permute-done.4 = f32[4,320,128]{2,1,0:T(8,128)S(1)} collective-permute-done((f32[4,320,128]{2,1,0:T(8,128)S(1)}, f32[4,320,128]{2,1,0:T(8,128)S(1)}, u32[]{:S(2)}, u32[]{:S(2)}) %collective-permute-start.4) | collective-permute-done | bytes 655392 | tf_op jit(solution)/shard_map/ppermute | solution.py:55
  26.1 4.3 %collective-permute-done.5 = f32[2,320,128]{2,1,0:T(8,128)S(1)} collective-permute-done((f32[2,320,128]{2,1,0:T(8,128)S(1)}, f32[2,320,128]{2,1,0:T(8,128)S(1)}, u32[]{:S(2)}, u32[]{:S(2)}) %collective-permute-start.5) | collective-permute-done | bytes 327712 | tf_op jit(solution)/shard_map/ppermute | solution.py:55
  30.5 2.4 %collective-permute-done.2 = f32[2,320,128]{2,1,0:T(8,128)} collective-permute-done((f32[2,320,128]{2,1,0:T(8,128)}, f32[2,320,128]{2,1,0:T(8,128)}, u32[]{:S(2)}, u32[]{:S(2)}) %collective-permute-start.2) | collective-permute-done | bytes 327712 | tf_op jit(solution)/shard_map/ppermute | solution.py:55
  34.0 2.4 %collective-permute-start.8 = (f32[320,128]{1,0:T(8,128)S(1)}, f32[320,128]{1,0:T(8,128)S(1)}, u32[]{:S(2)}, u32[]{:S(2)}) collective-permute-start(f32[320,128]{1,0:T(8,128)S(1)} %get-tuple-element.45), channel_id=1, source_target_pairs={{0,4},{1,129},{2,130},{3,7},{4,0},{5,133},{6,134},{7,3},{8,136},{9... | collective-permute-start | bytes 491528 | tf_op jit(solution)/shard_map/ppermute | solution.py:67
  37.1 2.3 %collective-permute-start.7 = (f32[320,128]{1,0:T(8,128)S(1)}, f32[320,128]{1,0:T(8,128)S(1)}, u32[]{:S(2)}, u32[]{:S(2)}) collective-permute-start(f32[320,128]{1,0:T(8,128)S(1)} %get-tuple-element.47), channel_id=1, source_target_pairs={{0,7},{1,192},{2,195},{3,0},{4,3},{5,196},{6,199},{7,4},{8,201},{9... | collective-permute-start | bytes 491528 | tf_op jit(solution)/shard_map/ppermute | solution.py:67
  40.1 2.5 %collective-permute-done.6 = f32[320,128]{1,0:T(8,128)S(1)} collective-permute-done((f32[320,128]{1,0:T(8,128)S(1)}, f32[320,128]{1,0:T(8,128)S(1)}, u32[]{:S(2)}, u32[]{:S(2)}) %collective-permute-start.6) | collective-permute-done | bytes 163872 | tf_op jit(solution)/shard_map/ppermute | solution.py:67
  42.7 1.7 %collective-permute-start.9 = (f32[160,128]{1,0:T(8,128)S(1)}, f32[160,128]{1,0:T(8,128)S(1)}, u32[]{:S(2)}, u32[]{:S(2)}) collective-permute-start(f32[160,128]{1,0:T(8,128)S(1)} %slice_select_fusion), channel_id=1, source_target_pairs={{0,9},{1,8},{2,11},{3,10},{4,13},{5,12},{6,15},{7,14},{8,1},{9,0},... | collective-permute-start | bytes 245768 | tf_op jit(solution)/shard_map/ppermute | solution.py:55
  44.4 2.9 %collective-permute-done.9 = f32[160,128]{1,0:T(8,128)S(1)} collective-permute-done((f32[160,128]{1,0:T(8,128)S(1)}, f32[160,128]{1,0:T(8,128)S(1)}, u32[]{:S(2)}, u32[]{:S(2)}) %collective-permute-start.9) | collective-permute-done | bytes 81952 | tf_op jit(solution)/shard_map/ppermute | solution.py:55
  47.3 6.7 %collective-permute-start.12 = (f32[160,128]{1,0:T(8,128)S(1)}, f32[160,128]{1,0:T(8,128)S(1)}, u32[]{:S(2)}, u32[]{:S(2)}) collective-permute-start(f32[160,128]{1,0:T(8,128)S(1)} %select_add_fusion), channel_id=1, source_target_pairs={{0,32},{1,33},{2,34},{3,35},{4,36},{5,37},{6,38},{7,39},{8,40},{9,... | collective-permute-start | bytes 245768 | tf_op jit(solution)/shard_map/ppermute | solution.py:55
  54.0 1.8 %collective-permute-start.10 = (f32[160,128]{1,0:T(8,128)S(1)}, f32[160,128]{1,0:T(8,128)S(1)}, u32[]{:S(2)}, u32[]{:S(2)}) collective-permute-start(f32[160,128]{1,0:T(8,128)S(1)} %select_add_fusion), channel_id=1, source_target_pairs={{0,25},{1,24},{2,27},{3,26},{4,29},{5,28},{6,31},{7,30},{8,17},{9,... | collective-permute-start | bytes 245768 | tf_op jit(solution)/shard_map/ppermute | solution.py:55
  56.5 5.5 %collective-permute-done.11 = f32[160,128]{1,0:T(8,128)S(1)} collective-permute-done((f32[160,128]{1,0:T(8,128)S(1)}, f32[160,128]{1,0:T(8,128)S(1)}, u32[]{:S(2)}, u32[]{:S(2)}) %collective-permute-start.11) | collective-permute-done | bytes 81952 | tf_op jit(solution)/shard_map/ppermute | solution.py:55
  63.3 3.3 %collective-permute-done.13 = f32[160,128]{1,0:T(8,128)S(1)} collective-permute-done((f32[160,128]{1,0:T(8,128)S(1)}, f32[160,128]{1,0:T(8,128)S(1)}, u32[]{:S(2)}, u32[]{:S(2)}) %collective-permute-start.13) | collective-permute-done | bytes 81952 | tf_op jit(solution)/shard_map/ppermute | solution.py:55
  66.6 2.1 %collective-permute-start.14 = (f32[320,128]{1,0:T(8,128)S(1)}, f32[320,128]{1,0:T(8,128)S(1)}, u32[]{:S(2)}, u32[]{:S(2)}) collective-permute-start(f32[320,128]{1,0:T(8,128)S(1)} %pad_maximum_fusion.2), channel_id=1, source_target_pairs={{0,7},{1,192},{2,195},{3,0},{4,3},{5,196},{6,199},{7,4},{8,201},{9... | collective-permute-start | bytes 491528 | tf_op jit(solution)/shard_map/ppermute | solution.py:67
  71.5 4.8 %collective-permute-done.15 = f32[320,128]{1,0:T(8,128)S(1)} collective-permute-done((f32[320,128]{1,0:T(8,128)S(1)}, f32[320,128]{1,0:T(8,128)S(1)}, u32[]{:S(2)}, u32[]{:S(2)}) %collective-permute-start.15) | collective-permute-done | bytes 163872 | tf_op jit(solution)/shard_map/ppermute | solution.py:67
  76.4 3.2 %collective-permute-start.19 = (f32[2,320,128]{2,1,0:T(8,128)S(1)}, f32[2,320,128]{2,1,0:T(8,128)S(1)}, u32[]{:S(2)}, u32[]{:S(2)}) collective-permute-start(f32[2,320,128]{2,1,0:T(8,128)S(1)} %get-tuple-element.43), channel_id=1, source_target_pairs={{0,193},{1,6},{2,5},{3,194},{4,197},{5,2},{6,1},{7,198},{8,15},{9,... | collective-permute-start | bytes 983048 | tf_op jit(solution)/shard_map/ppermute | solution.py:55
  79.6 4.8 %collective-permute-done.19 = f32[2,320,128]{2,1,0:T(8,128)S(1)} collective-permute-done((f32[2,320,128]{2,1,0:T(8,128)S(1)}, f32[2,320,128]{2,1,0:T(8,128)S(1)}, u32[]{:S(2)}, u32[]{:S(2)}) %collective-permute-start.19) | collective-permute-done | bytes 327712 | tf_op jit(solution)/shard_map/ppermute | solution.py:55
  84.5 1.6 %collective-permute-done.17 = f32[2,320,128]{2,1,0:T(8,128)S(1)} collective-permute-done((f32[2,320,128]{2,1,0:T(8,128)S(1)}, f32[2,320,128]{2,1,0:T(8,128)S(1)}, u32[]{:S(2)}, u32[]{:S(2)}) %collective-permute-start.17) | collective-permute-done | bytes 327712 | tf_op jit(solution)/shard_map/ppermute | solution.py:55
  86.2 1.5 %collective-permute-start.18 = (f32[4,320,128]{2,1,0:T(8,128)S(1)}, f32[4,320,128]{2,1,0:T(8,128)S(1)}, u32[]{:S(2)}, u32[]{:S(2)}) collective-permute-start(f32[4,320,128]{2,1,0:T(8,128)S(1)} %pad_maximum_fusion.piece), channel_id=1, source_target_pairs={{0,193},{1,6},{2,5},{3,194},{4,197},{5,2},{6,1},{7,198},{8,15},{9,... | collective-permute-start | bytes 1966088 | tf_op jit(solution)/shard_map/ppermute | solution.py:55
  90.3 4.5 %collective-permute-done.20.piece = f32[4,320,128]{2,1,0:T(8,128)S(1)} collective-permute-done((f32[4,320,128]{2,1,0:T(8,128)S(1)}, f32[4,320,128]{2,1,0:T(8,128)S(1)}, u32[]{:S(2)}, u32[]{:S(2)}) %collective-permute-start.20) | collective-permute-done | bytes 655392 | tf_op jit(solution)/shard_map/ppermute | solution.py:55
  101.5 14.4 %shard_map.34 = (bf16[320,960]{1,0:T(8,128)(2,1)S(1)}, f32[320,320]{1,0:T(8,128)S(1)}) custom-call(s32[1]{0:T(128)} %bitcast.id_ref, f32[2,320,384]{2,1,0:T(8,128)S(1)} %get-tuple-element.32.own, f32[2,320,384]{2,1,0:T(8,128)S(1)} %collective-permute-done.21.other), custom_call_target="tpu_custom_call" | custom-call | flops 18790481920 | bytes 4194304 | tf_op jit(solution)/shard_map/pallas_call | solution.py:165
  115.9 6.6 %shard_map.35 = f32[320,512]{1,0:T(8,128)} custom-call(s32[1]{0:T(128)} %bitcast.id_ref, bf16[512,4096]{1,0:T(8,128)(2,1)S(1)} %copy-done.2, bf16[320,960]{1,0:T(8,128)(2,1)S(1)} %get-tuple-element.33.basis_map, f32[320,320]{1,0:T(8,128)S(1)} %get-tuple-element.34.inverse_c, bf16[960,512]{1,0:T(8,128)(2,1)S(1)} %get-tuple-element.35.refs_0_, ...), custom_call_target="tpu_custom_call" | custom-call | flops 5368709120 | bytes 4194304 | tf_op jit(solution)/shard_map/pallas_call | solution.py:165
  (63 shorter events, 22.7 us)
Async XLA Ops:
  6.0 6.0 %collective-permute-start.3 = (f32[8,320,128]{2,1,0:T(8,128)S(1)}, f32[8,320,128]{2,1,0:T(8,128)S(1)}, u32[]{:S(2)}, u32[]{:S(2)}) collective-permute-start(f32[8,320,128]{2,1,0:T(8,128)S(1)} %get-tuple-element.27), channel_id=1, source_target_pairs={{0,1},{1,0},{2,3},{3,2},{4,5},{5,4},{6,7},{7,6},{8,9},{9,8},{10,11... | collective-permute-start | bytes 3932168 | tf_op jit(solution)/shard_map/ppermute | solution.py:42
  12.1 11.3 %collective-permute-start.4 = (f32[4,320,128]{2,1,0:T(8,128)S(1)}, f32[4,320,128]{2,1,0:T(8,128)S(1)}, u32[]{:S(2)}, u32[]{:S(2)}) collective-permute-start(f32[4,320,128]{2,1,0:T(8,128)S(1)} %get-tuple-element.40), channel_id=1, source_target_pairs={{0,193},{1,6},{2,5},{3,194},{4,197},{5,2},{6,1},{7,198},{8,15},{9,... | collective-permute-start | bytes 1966088 | tf_op jit(solution)/shard_map/ppermute | solution.py:55
  14.0 10.1 %collective-permute-start.1 = (f32[4,320,128]{2,1,0:T(8,128)S(1)}, f32[4,320,128]{2,1,0:T(8,128)S(1)}, u32[]{:S(2)}, u32[]{:S(2)}) collective-permute-start(f32[4,320,128]{2,1,0:T(8,128)S(1)} %get-tuple-element.42), channel_id=1, source_target_pairs={{0,65},{1,2},{2,1},{3,66},{4,69},{5,6},{6,5},{7,70},{8,11},{9,72},... | collective-permute-start | bytes 1966088 | tf_op jit(solution)/shard_map/ppermute | solution.py:55
  23.5 7.0 %collective-permute-start.5 = (f32[2,320,128]{2,1,0:T(8,128)S(1)}, f32[2,320,128]{2,1,0:T(8,128)S(1)}, u32[]{:S(2)}, u32[]{:S(2)}) collective-permute-start(f32[2,320,128]{2,1,0:T(8,128)S(1)} %slice_add_fusion.4), channel_id=1, source_target_pairs={{0,65},{1,2},{2,1},{3,66},{4,69},{5,6},{6,5},{7,70},{8,11},{9,72},... | collective-permute-start | bytes 983048 | tf_op jit(solution)/shard_map/ppermute | solution.py:55
  24.8 8.0 %collective-permute-start.2 = (f32[2,320,128]{2,1,0:T(8,128)}, f32[2,320,128]{2,1,0:T(8,128)}, u32[]{:S(2)}, u32[]{:S(2)}) collective-permute-start(f32[2,320,128]{2,1,0:T(8,128)} %slice_add_fusion.6), channel_id=1, source_target_pairs={{0,193},{1,6},{2,5},{3,194},{4,197},{5,2},{6,1},{7,198},{8,15},{9,... | collective-permute-start | bytes 983048 | tf_op jit(solution)/shard_map/ppermute | solution.py:55
  34.0 6.1 %collective-permute-start.8 = (f32[320,128]{1,0:T(8,128)S(1)}, f32[320,128]{1,0:T(8,128)S(1)}, u32[]{:S(2)}, u32[]{:S(2)}) collective-permute-start(f32[320,128]{1,0:T(8,128)S(1)} %get-tuple-element.45), channel_id=1, source_target_pairs={{0,4},{1,129},{2,130},{3,7},{4,0},{5,133},{6,134},{7,3},{8,136},{9... | collective-permute-start | bytes 491528 | tf_op jit(solution)/shard_map/ppermute | solution.py:67
  36.4 6.2 %collective-permute-start.6 = (f32[320,128]{1,0:T(8,128)S(1)}, f32[320,128]{1,0:T(8,128)S(1)}, u32[]{:S(2)}, u32[]{:S(2)}) collective-permute-start(f32[320,128]{1,0:T(8,128)S(1)} %get-tuple-element.46), channel_id=1, source_target_pairs={{0,3},{1,64},{2,67},{3,4},{4,7},{5,68},{6,71},{7,0},{8,73},{9,10},... | collective-permute-start | bytes 491528 | tf_op jit(solution)/shard_map/ppermute | solution.py:67
  37.1 5.6 %collective-permute-start.7 = (f32[320,128]{1,0:T(8,128)S(1)}, f32[320,128]{1,0:T(8,128)S(1)}, u32[]{:S(2)}, u32[]{:S(2)}) collective-permute-start(f32[320,128]{1,0:T(8,128)S(1)} %get-tuple-element.47), channel_id=1, source_target_pairs={{0,7},{1,192},{2,195},{3,0},{4,3},{5,196},{6,199},{7,4},{8,201},{9... | collective-permute-start | bytes 491528 | tf_op jit(solution)/shard_map/ppermute | solution.py:67
  42.7 4.6 %collective-permute-start.9 = (f32[160,128]{1,0:T(8,128)S(1)}, f32[160,128]{1,0:T(8,128)S(1)}, u32[]{:S(2)}, u32[]{:S(2)}) collective-permute-start(f32[160,128]{1,0:T(8,128)S(1)} %slice_select_fusion), channel_id=1, source_target_pairs={{0,9},{1,8},{2,11},{3,10},{4,13},{5,12},{6,15},{7,14},{8,1},{9,0},... | collective-permute-start | bytes 245768 | tf_op jit(solution)/shard_map/ppermute | solution.py:55
  47.3 9.2 %collective-permute-start.12 = (f32[160,128]{1,0:T(8,128)S(1)}, f32[160,128]{1,0:T(8,128)S(1)}, u32[]{:S(2)}, u32[]{:S(2)}) collective-permute-start(f32[160,128]{1,0:T(8,128)S(1)} %select_add_fusion), channel_id=1, source_target_pairs={{0,32},{1,33},{2,34},{3,35},{4,36},{5,37},{6,38},{7,39},{8,40},{9,... | collective-permute-start | bytes 245768 | tf_op jit(solution)/shard_map/ppermute | solution.py:55
  54.0 8.0 %collective-permute-start.11 = (f32[160,128]{1,0:T(8,128)S(1)}, f32[160,128]{1,0:T(8,128)S(1)}, u32[]{:S(2)}, u32[]{:S(2)}) collective-permute-start(f32[160,128]{1,0:T(8,128)S(1)} %select_add_fusion), channel_id=1, source_target_pairs={{0,57},{1,56},{2,59},{3,58},{4,61},{5,60},{6,63},{7,62},{8,49},{9,... | collective-permute-start | bytes 245768 | tf_op jit(solution)/shard_map/ppermute | solution.py:55
  54.0 8.0 %collective-permute-start.10 = (f32[160,128]{1,0:T(8,128)S(1)}, f32[160,128]{1,0:T(8,128)S(1)}, u32[]{:S(2)}, u32[]{:S(2)}) collective-permute-start(f32[160,128]{1,0:T(8,128)S(1)} %select_add_fusion), channel_id=1, source_target_pairs={{0,25},{1,24},{2,27},{3,26},{4,29},{5,28},{6,31},{7,30},{8,17},{9,... | collective-permute-start | bytes 245768 | tf_op jit(solution)/shard_map/ppermute | solution.py:55
  62.0 4.5 %collective-permute-start.13 = (f32[160,128]{1,0:T(8,128)S(1)}, f32[160,128]{1,0:T(8,128)S(1)}, u32[]{:S(2)}, u32[]{:S(2)}) collective-permute-start(f32[160,128]{1,0:T(8,128)S(1)} %add_add_fusion), channel_id=1, source_target_pairs={{0,9},{1,8},{2,11},{3,10},{4,13},{5,12},{6,15},{7,14},{8,1},{9,0},... | collective-permute-start | bytes 245768 | tf_op jit(solution)/shard_map/ppermute | solution.py:55
  66.6 4.8 %collective-permute-start.14 = (f32[320,128]{1,0:T(8,128)S(1)}, f32[320,128]{1,0:T(8,128)S(1)}, u32[]{:S(2)}, u32[]{:S(2)}) collective-permute-start(f32[320,128]{1,0:T(8,128)S(1)} %pad_maximum_fusion.2), channel_id=1, source_target_pairs={{0,7},{1,192},{2,195},{3,0},{4,3},{5,196},{6,199},{7,4},{8,201},{9... | collective-permute-start | bytes 491528 | tf_op jit(solution)/shard_map/ppermute | solution.py:67
  68.8 7.5 %collective-permute-start.15 = (f32[320,128]{1,0:T(8,128)S(1)}, f32[320,128]{1,0:T(8,128)S(1)}, u32[]{:S(2)}, u32[]{:S(2)}) collective-permute-start(f32[320,128]{1,0:T(8,128)S(1)} %pad_maximum_fusion.2), channel_id=1, source_target_pairs={{0,3},{1,64},{2,67},{3,4},{4,7},{5,68},{6,71},{7,0},{8,73},{9,10},... | collective-permute-start | bytes 491528 | tf_op jit(solution)/shard_map/ppermute | solution.py:67
  68.8 7.5 %collective-permute-start.16 = (f32[320,128]{1,0:T(8,128)S(1)}, f32[320,128]{1,0:T(8,128)S(1)}, u32[]{:S(2)}, u32[]{:S(2)}) collective-permute-start(f32[320,128]{1,0:T(8,128)S(1)} %pad_maximum_fusion.2), channel_id=1, source_target_pairs={{0,4},{1,129},{2,130},{3,7},{4,0},{5,133},{6,134},{7,3},{8,136},{9... | collective-permute-start | bytes 491528 | tf_op jit(solution)/shard_map/ppermute | solution.py:67
  76.4 8.0 %collective-permute-start.19 = (f32[2,320,128]{2,1,0:T(8,128)S(1)}, f32[2,320,128]{2,1,0:T(8,128)S(1)}, u32[]{:S(2)}, u32[]{:S(2)}) collective-permute-start(f32[2,320,128]{2,1,0:T(8,128)S(1)} %get-tuple-element.43), channel_id=1, source_target_pairs={{0,193},{1,6},{2,5},{3,194},{4,197},{5,2},{6,1},{7,198},{8,15},{9,... | collective-permute-start | bytes 983048 | tf_op jit(solution)/shard_map/ppermute | solution.py:55
  79.6 6.5 %collective-permute-start.17 = (f32[2,320,128]{2,1,0:T(8,128)S(1)}, f32[2,320,128]{2,1,0:T(8,128)S(1)}, u32[]{:S(2)}, u32[]{:S(2)}) collective-permute-start(f32[2,320,128]{2,1,0:T(8,128)S(1)} %get-tuple-element.44), channel_id=1, source_target_pairs={{0,65},{1,2},{2,1},{3,66},{4,69},{5,6},{6,5},{7,70},{8,11},{9,72},... | collective-permute-start | bytes 983048 | tf_op jit(solution)/shard_map/ppermute | solution.py:55
  84.4 10.4 %collective-permute-start.20 = (f32[4,320,128]{2,1,0:T(8,128)S(1)}, f32[4,320,128]{2,1,0:T(8,128)S(1)}, u32[]{:S(2)}, u32[]{:S(2)}) collective-permute-start(f32[4,320,128]{2,1,0:T(8,128)S(1)} %pad_maximum_fusion.1.piece), channel_id=1, source_target_pairs={{0,65},{1,2},{2,1},{3,66},{4,69},{5,6},{6,5},{7,70},{8,11},{9,72},... | collective-permute-start | bytes 1966088 | tf_op jit(solution)/shard_map/ppermute | solution.py:55
  86.2 11.3 %collective-permute-start.18 = (f32[4,320,128]{2,1,0:T(8,128)S(1)}, f32[4,320,128]{2,1,0:T(8,128)S(1)}, u32[]{:S(2)}, u32[]{:S(2)}) collective-permute-start(f32[4,320,128]{2,1,0:T(8,128)S(1)} %pad_maximum_fusion.piece), channel_id=1, source_target_pairs={{0,193},{1,6},{2,5},{3,194},{4,197},{5,2},{6,1},{7,198},{8,15},{9,... | collective-permute-start | bytes 1966088 | tf_op jit(solution)/shard_map/ppermute | solution.py:55
  99.1 16.8 %collective-permute-start.23 = (bf16[960,512]{1,0:T(8,128)(2,1)S(1)}, bf16[960,512]{1,0:T(8,128)(2,1)S(1)}, u32[]{:S(2)}, u32[]{:S(2)}) collective-permute-start(bf16[960,512]{1,0:T(8,128)(2,1)S(1)} %get-tuple-element.36.refs_1_), channel_id=1, source_target_pairs={{0,1},{1,0},{2,3},{3,2},{4,5},{5,4},{6,7},{7,6},{8,9},{9,8},{10,11... | collective-permute-start | bytes 2949128 | tf_op jit(solution)/shard_map/ppermute | solution.py:42
  99.4 16.5 %collective-permute-start.22 = (bf16[960,512]{1,0:T(8,128)(2,1)S(1)}, bf16[960,512]{1,0:T(8,128)(2,1)S(1)}, u32[]{:S(2)}, u32[]{:S(2)}) collective-permute-start(bf16[960,512]{1,0:T(8,128)(2,1)S(1)} %get-tuple-element.35.refs_0_), channel_id=1, source_target_pairs={{0,1},{1,0},{2,3},{3,2},{4,5},{5,4},{6,7},{7,6},{8,9},{9,8},{10,11... | collective-permute-start | bytes 2949128 | tf_op jit(solution)/shard_map/ppermute | solution.py:42
  99.6 16.3 %collective-permute-start.25 = (bf16[960,512]{1,0:T(8,128)(2,1)S(1)}, bf16[960,512]{1,0:T(8,128)(2,1)S(1)}, u32[]{:S(2)}, u32[]{:S(2)}) collective-permute-start(bf16[960,512]{1,0:T(8,128)(2,1)S(1)} %get-tuple-element.38.refs_3_), channel_id=1, source_target_pairs={{0,1},{1,0},{2,3},{3,2},{4,5},{5,4},{6,7},{7,6},{8,9},{9,8},{10,11... | collective-permute-start | bytes 2949128 | tf_op jit(solution)/shard_map/ppermute | solution.py:42
  99.9 16.0 %collective-permute-start.24 = (bf16[960,512]{1,0:T(8,128)(2,1)S(1)}, bf16[960,512]{1,0:T(8,128)(2,1)S(1)}, u32[]{:S(2)}, u32[]{:S(2)}) collective-permute-start(bf16[960,512]{1,0:T(8,128)(2,1)S(1)} %get-tuple-element.37.refs_2_), channel_id=1, source_target_pairs={{0,1},{1,0},{2,3},{3,2},{4,5},{5,4},{6,7},{7,6},{8,9},{9,8},{10,11... | collective-permute-start | bytes 2949128 | tf_op jit(solution)/shard_map/ppermute | solution.py:42
  (5 other events, 40.6 us)

commit v2 on v1

--- a/solution.py
+++ b/solution.py
@@ -374,15 +374,8 @@
 def final_kernel(members, id_ref, features, basis_map, inverse_c, *refs):
     terms, (result, coeffs) = refs[:-2], refs[-2:]
     place = coordinates(id_ref[0])
-    part = WIDTH // 2
-
-    @pl.loop(0, 2)
-    def _(n):
-        here = pl.ds(pl.multiple_of(n * part, part), part)
-        for term, member in zip(terms, members):
-            start = pl.multiple_of(columns_of(place, *member).start + n * part, part)
-            coeffs[:, pl.ds(start, part)] = dot(basis_map[...], term[:, here]).astype(BF16)
-
+    for term, member in zip(terms, members):
+        coeffs[:, columns_of(place, *member)] = dot(basis_map[...], term[...]).astype(BF16)
     projected = dot_nt(coeffs[...], features[...])
     result[...] = dot_three(inverse_c[...], projected)
 

time: 123 us -> 122 us (level)
  no operation moved by 1% of the time
where the time goes in v2:
time: 122 us
  waiting for transfers between devices  53.3 us (44%)
  Pallas kernels  33.5 us (27%)
  starting transfers between devices  32.3 us (26%)
  other arithmetic  2.47 us (2%)
    ppermute x13, waiting for transfers between devices, exchange(): return lax.ppermute(block, 'rows', pairs)  41 us
    pallas_call x8, Pallas kernels, call(): pl.pallas_call(kernel, out_shape=[jax.ShapeDtypeStruct(shape, dtype) for...  33.5 us
    ppermute x13, starting transfers between devices, exchange(): return lax.ppermute(block, 'rows', pairs)  18.9 us
    ppermute x6, waiting for transfers between devices, shifted(): return lax.ppermute(block, 'rows', pairs)  9.42 us
    ppermute x6, starting transfers between devices, shifted(): return lax.ppermute(block, 'rows', pairs)  8.72 us
    ppermute x7, starting transfers between devices, across(): lax.ppermute(block, 'rows', [(i, i ^ 1) for i in range(lax.axis_size('row...  4.71 us
    ppermute x7, waiting for transfers between devices, across(): lax.ppermute(block, 'rows', [(i, i ^ 1) for i in range(lax.axis_size('row...  2.87 us
  transfers between devices with their start and end apart: 26, of which 19 were waited for; matrix products, arithmetic and copies ran while one was open for 1% of the time, Pallas kernels for 16%

profile of v2, /device:TPU:1, one launch (start us, length us, event | category | flops | bytes accessed | tf_op | source)
XLA Modules:
  0.0 122.0 jit_solution(12427441232427875949)
XLA Ops:
  0.0 6.0 %shard_map.28 = (bf16[640,512]{1,0:T(8,128)(2,1)S(1)}, f32[8,320,128]{2,1,0:T(8,128)S(1)}, f32[8,320,128]{2,1,0:T(8,128)S(1)}) custom-call(s32[1]{0:T(128)} %bitcast.id_ref, bf16[512,4096]{1,0:T(8,128)(2,1)} %features.3, bf16[320,4096]{1,0:T(8,128)(2,1)} %bitcast.23), custom_call_target="tpu_custom_call" | custom-call | flops 2684354560 | bytes 4194304 | tf_op jit(solution)/shard_map/pallas_call | solution.py:165
  6.0 3.3 %collective-permute-start.3 = (f32[8,320,128]{2,1,0:T(8,128)S(1)}, f32[8,320,128]{2,1,0:T(8,128)S(1)}, u32[]{:S(2)}, u32[]{:S(2)}) collective-permute-start(f32[8,320,128]{2,1,0:T(8,128)S(1)} %get-tuple-element.27), channel_id=1, source_target_pairs={{0,1},{1,0},{2,3},{3,2},{4,5},{5,4},{6,7},{7,6},{8,9},{9,8},{10,11... | collective-permute-start | bytes 3932168 | tf_op jit(solution)/shard_map/ppermute | solution.py:42
  9.4 1.7 %shard_map.29 = (f32[4,320,128]{2,1,0:T(8,128)S(1)}, f32[4,320,128]{2,1,0:T(8,128)S(1)}, f32[4,320,128]{2,1,0:T(8,128)S(1)}, f32[4,320,128]{2,1,0:T(8,128)S(1)}) custom-call(s32[1]{0:T(128)} %bitcast.id_ref, bf16[512,4096]{1,0:T(8,128)(2,1)S(1)} %copy-done.1, bf16[640,512]{1,0:T(8,128)(2,1)S(1)} %get-tuple-element.22.sketches), custom_call_target="tpu_custom_call" | custom-call | flops 1342177280 | bytes 4194304 | tf_op jit(solution)/shard_map/pallas_call | solution.py:165
  14.1 9.3 %collective-permute-done.4 = f32[4,320,128]{2,1,0:T(8,128)S(1)} collective-permute-done((f32[4,320,128]{2,1,0:T(8,128)S(1)}, f32[4,320,128]{2,1,0:T(8,128)S(1)}, u32[]{:S(2)}, u32[]{:S(2)}) %collective-permute-start.4) | collective-permute-done | bytes 655392 | tf_op jit(solution)/shard_map/ppermute | solution.py:55
  26.1 4.3 %collective-permute-done.5 = f32[2,320,128]{2,1,0:T(8,128)S(1)} collective-permute-done((f32[2,320,128]{2,1,0:T(8,128)S(1)}, f32[2,320,128]{2,1,0:T(8,128)S(1)}, u32[]{:S(2)}, u32[]{:S(2)}) %collective-permute-start.5) | collective-permute-done | bytes 327712 | tf_op jit(solution)/shard_map/ppermute | solution.py:55
  30.5 2.4 %collective-permute-done.2 = f32[2,320,128]{2,1,0:T(8,128)} collective-permute-done((f32[2,320,128]{2,1,0:T(8,128)}, f32[2,320,128]{2,1,0:T(8,128)}, u32[]{:S(2)}, u32[]{:S(2)}) %collective-permute-start.2) | collective-permute-done | bytes 327712 | tf_op jit(solution)/shard_map/ppermute | solution.py:55
  34.0 2.4 %collective-permute-start.8 = (f32[320,128]{1,0:T(8,128)S(1)}, f32[320,128]{1,0:T(8,128)S(1)}, u32[]{:S(2)}, u32[]{:S(2)}) collective-permute-start(f32[320,128]{1,0:T(8,128)S(1)} %get-tuple-element.45), channel_id=1, source_target_pairs={{0,4},{1,129},{2,130},{3,7},{4,0},{5,133},{6,134},{7,3},{8,136},{9... | collective-permute-start | bytes 491528 | tf_op jit(solution)/shard_map/ppermute | solution.py:67
  37.1 2.3 %collective-permute-start.7 = (f32[320,128]{1,0:T(8,128)S(1)}, f32[320,128]{1,0:T(8,128)S(1)}, u32[]{:S(2)}, u32[]{:S(2)}) collective-permute-start(f32[320,128]{1,0:T(8,128)S(1)} %get-tuple-element.47), channel_id=1, source_target_pairs={{0,7},{1,192},{2,195},{3,0},{4,3},{5,196},{6,199},{7,4},{8,201},{9... | collective-permute-start | bytes 491528 | tf_op jit(solution)/shard_map/ppermute | solution.py:67
  40.1 2.5 %collective-permute-done.6 = f32[320,128]{1,0:T(8,128)S(1)} collective-permute-done((f32[320,128]{1,0:T(8,128)S(1)}, f32[320,128]{1,0:T(8,128)S(1)}, u32[]{:S(2)}, u32[]{:S(2)}) %collective-permute-start.6) | collective-permute-done | bytes 163872 | tf_op jit(solution)/shard_map/ppermute | solution.py:67
  42.7 1.7 %collective-permute-start.9 = (f32[160,128]{1,0:T(8,128)S(1)}, f32[160,128]{1,0:T(8,128)S(1)}, u32[]{:S(2)}, u32[]{:S(2)}) collective-permute-start(f32[160,128]{1,0:T(8,128)S(1)} %slice_select_fusion), channel_id=1, source_target_pairs={{0,9},{1,8},{2,11},{3,10},{4,13},{5,12},{6,15},{7,14},{8,1},{9,0},... | collective-permute-start | bytes 245768 | tf_op jit(solution)/shard_map/ppermute | solution.py:55
  44.4 2.9 %collective-permute-done.9 = f32[160,128]{1,0:T(8,128)S(1)} collective-permute-done((f32[160,128]{1,0:T(8,128)S(1)}, f32[160,128]{1,0:T(8,128)S(1)}, u32[]{:S(2)}, u32[]{:S(2)}) %collective-permute-start.9) | collective-permute-done | bytes 81952 | tf_op jit(solution)/shard_map/ppermute | solution.py:55
  47.3 6.7 %collective-permute-start.12 = (f32[160,128]{1,0:T(8,128)S(1)}, f32[160,128]{1,0:T(8,128)S(1)}, u32[]{:S(2)}, u32[]{:S(2)}) collective-permute-start(f32[160,128]{1,0:T(8,128)S(1)} %select_add_fusion), channel_id=1, source_target_pairs={{0,32},{1,33},{2,34},{3,35},{4,36},{5,37},{6,38},{7,39},{8,40},{9,... | collective-permute-start | bytes 245768 | tf_op jit(solution)/shard_map/ppermute | solution.py:55
  54.0 1.8 %collective-permute-start.10 = (f32[160,128]{1,0:T(8,128)S(1)}, f32[160,128]{1,0:T(8,128)S(1)}, u32[]{:S(2)}, u32[]{:S(2)}) collective-permute-start(f32[160,128]{1,0:T(8,128)S(1)} %select_add_fusion), channel_id=1, source_target_pairs={{0,25},{1,24},{2,27},{3,26},{4,29},{5,28},{6,31},{7,30},{8,17},{9,... | collective-permute-start | bytes 245768 | tf_op jit(solution)/shard_map/ppermute | solution.py:55
  56.5 5.5 %collective-permute-done.11 = f32[160,128]{1,0:T(8,128)S(1)} collective-permute-done((f32[160,128]{1,0:T(8,128)S(1)}, f32[160,128]{1,0:T(8,128)S(1)}, u32[]{:S(2)}, u32[]{:S(2)}) %collective-permute-start.11) | collective-permute-done | bytes 81952 | tf_op jit(solution)/shard_map/ppermute | solution.py:55
  63.3 3.3 %collective-permute-done.13 = f32[160,128]{1,0:T(8,128)S(1)} collective-permute-done((f32[160,128]{1,0:T(8,128)S(1)}, f32[160,128]{1,0:T(8,128)S(1)}, u32[]{:S(2)}, u32[]{:S(2)}) %collective-permute-start.13) | collective-permute-done | bytes 81952 | tf_op jit(solution)/shard_map/ppermute | solution.py:55
  66.6 2.1 %collective-permute-start.14 = (f32[320,128]{1,0:T(8,128)S(1)}, f32[320,128]{1,0:T(8,128)S(1)}, u32[]{:S(2)}, u32[]{:S(2)}) collective-permute-start(f32[320,128]{1,0:T(8,128)S(1)} %pad_maximum_fusion.2), channel_id=1, source_target_pairs={{0,7},{1,192},{2,195},{3,0},{4,3},{5,196},{6,199},{7,4},{8,201},{9... | collective-permute-start | bytes 491528 | tf_op jit(solution)/shard_map/ppermute | solution.py:67
  71.5 4.8 %collective-permute-done.15 = f32[320,128]{1,0:T(8,128)S(1)} collective-permute-done((f32[320,128]{1,0:T(8,128)S(1)}, f32[320,128]{1,0:T(8,128)S(1)}, u32[]{:S(2)}, u32[]{:S(2)}) %collective-permute-start.15) | collective-permute-done | bytes 163872 | tf_op jit(solution)/shard_map/ppermute | solution.py:67
  76.4 3.2 %collective-permute-start.19 = (f32[2,320,128]{2,1,0:T(8,128)S(1)}, f32[2,320,128]{2,1,0:T(8,128)S(1)}, u32[]{:S(2)}, u32[]{:S(2)}) collective-permute-start(f32[2,320,128]{2,1,0:T(8,128)S(1)} %get-tuple-element.43), channel_id=1, source_target_pairs={{0,193},{1,6},{2,5},{3,194},{4,197},{5,2},{6,1},{7,198},{8,15},{9,... | collective-permute-start | bytes 983048 | tf_op jit(solution)/shard_map/ppermute | solution.py:55
  79.6 4.8 %collective-permute-done.19 = f32[2,320,128]{2,1,0:T(8,128)S(1)} collective-permute-done((f32[2,320,128]{2,1,0:T(8,128)S(1)}, f32[2,320,128]{2,1,0:T(8,128)S(1)}, u32[]{:S(2)}, u32[]{:S(2)}) %collective-permute-start.19) | collective-permute-done | bytes 327712 | tf_op jit(solution)/shard_map/ppermute | solution.py:55
  84.5 1.6 %collective-permute-done.17 = f32[2,320,128]{2,1,0:T(8,128)S(1)} collective-permute-done((f32[2,320,128]{2,1,0:T(8,128)S(1)}, f32[2,320,128]{2,1,0:T(8,128)S(1)}, u32[]{:S(2)}, u32[]{:S(2)}) %collective-permute-start.17) | collective-permute-done | bytes 327712 | tf_op jit(solution)/shard_map/ppermute | solution.py:55
  86.2 1.5 %collective-permute-start.18 = (f32[4,320,128]{2,1,0:T(8,128)S(1)}, f32[4,320,128]{2,1,0:T(8,128)S(1)}, u32[]{:S(2)}, u32[]{:S(2)}) collective-permute-start(f32[4,320,128]{2,1,0:T(8,128)S(1)} %pad_maximum_fusion.piece), channel_id=1, source_target_pairs={{0,193},{1,6},{2,5},{3,194},{4,197},{5,2},{6,1},{7,198},{8,15},{9,... | collective-permute-start | bytes 1966088 | tf_op jit(solution)/shard_map/ppermute | solution.py:55
  90.3 4.5 %collective-permute-done.20.piece = f32[4,320,128]{2,1,0:T(8,128)S(1)} collective-permute-done((f32[4,320,128]{2,1,0:T(8,128)S(1)}, f32[4,320,128]{2,1,0:T(8,128)S(1)}, u32[]{:S(2)}, u32[]{:S(2)}) %collective-permute-start.20) | collective-permute-done | bytes 655392 | tf_op jit(solution)/shard_map/ppermute | solution.py:55
  101.5 14.4 %shard_map.34 = (bf16[320,960]{1,0:T(8,128)(2,1)S(1)}, f32[320,320]{1,0:T(8,128)S(1)}) custom-call(s32[1]{0:T(128)} %bitcast.id_ref, f32[2,320,384]{2,1,0:T(8,128)S(1)} %get-tuple-element.32.own, f32[2,320,384]{2,1,0:T(8,128)S(1)} %collective-permute-done.21.other), custom_call_target="tpu_custom_call" | custom-call | flops 18790481920 | bytes 4194304 | tf_op jit(solution)/shard_map/pallas_call | solution.py:165
  115.9 6.1 %shard_map.35 = f32[320,512]{1,0:T(8,128)} custom-call(s32[1]{0:T(128)} %bitcast.id_ref, bf16[512,4096]{1,0:T(8,128)(2,1)S(1)} %copy-done.2, bf16[320,960]{1,0:T(8,128)(2,1)S(1)} %get-tuple-element.33.basis_map, f32[320,320]{1,0:T(8,128)S(1)} %get-tuple-element.34.inverse_c, bf16[960,512]{1,0:T(8,128)(2,1)S(1)} %get-tuple-element.35.refs_0_, ...), custom_call_target="tpu_custom_call" | custom-call | flops 5368709120 | bytes 4194304 | tf_op jit(solution)/shard_map/pallas_call | solution.py:165
  (63 shorter events, 22.7 us)
Async XLA Ops:
  6.0 6.0 %collective-permute-start.3 = (f32[8,320,128]{2,1,0:T(8,128)S(1)}, f32[8,320,128]{2,1,0:T(8,128)S(1)}, u32[]{:S(2)}, u32[]{:S(2)}) collective-permute-start(f32[8,320,128]{2,1,0:T(8,128)S(1)} %get-tuple-element.27), channel_id=1, source_target_pairs={{0,1},{1,0},{2,3},{3,2},{4,5},{5,4},{6,7},{7,6},{8,9},{9,8},{10,11... | collective-permute-start | bytes 3932168 | tf_op jit(solution)/shard_map/ppermute | solution.py:42
  12.1 11.3 %collective-permute-start.4 = (f32[4,320,128]{2,1,0:T(8,128)S(1)}, f32[4,320,128]{2,1,0:T(8,128)S(1)}, u32[]{:S(2)}, u32[]{:S(2)}) collective-permute-start(f32[4,320,128]{2,1,0:T(8,128)S(1)} %get-tuple-element.40), channel_id=1, source_target_pairs={{0,193},{1,6},{2,5},{3,194},{4,197},{5,2},{6,1},{7,198},{8,15},{9,... | collective-permute-start | bytes 1966088 | tf_op jit(solution)/shard_map/ppermute | solution.py:55
  14.0 10.1 %collective-permute-start.1 = (f32[4,320,128]{2,1,0:T(8,128)S(1)}, f32[4,320,128]{2,1,0:T(8,128)S(1)}, u32[]{:S(2)}, u32[]{:S(2)}) collective-permute-start(f32[4,320,128]{2,1,0:T(8,128)S(1)} %get-tuple-element.42), channel_id=1, source_target_pairs={{0,65},{1,2},{2,1},{3,66},{4,69},{5,6},{6,5},{7,70},{8,11},{9,72},... | collective-permute-start | bytes 1966088 | tf_op jit(solution)/shard_map/ppermute | solution.py:55
  23.5 7.0 %collective-permute-start.5 = (f32[2,320,128]{2,1,0:T(8,128)S(1)}, f32[2,320,128]{2,1,0:T(8,128)S(1)}, u32[]{:S(2)}, u32[]{:S(2)}) collective-permute-start(f32[2,320,128]{2,1,0:T(8,128)S(1)} %slice_add_fusion.4), channel_id=1, source_target_pairs={{0,65},{1,2},{2,1},{3,66},{4,69},{5,6},{6,5},{7,70},{8,11},{9,72},... | collective-permute-start | bytes 983048 | tf_op jit(solution)/shard_map/ppermute | solution.py:55
  24.8 8.0 %collective-permute-start.2 = (f32[2,320,128]{2,1,0:T(8,128)}, f32[2,320,128]{2,1,0:T(8,128)}, u32[]{:S(2)}, u32[]{:S(2)}) collective-permute-start(f32[2,320,128]{2,1,0:T(8,128)} %slice_add_fusion.6), channel_id=1, source_target_pairs={{0,193},{1,6},{2,5},{3,194},{4,197},{5,2},{6,1},{7,198},{8,15},{9,... | collective-permute-start | bytes 983048 | tf_op jit(solution)/shard_map/ppermute | solution.py:55
  34.0 6.1 %collective-permute-start.8 = (f32[320,128]{1,0:T(8,128)S(1)}, f32[320,128]{1,0:T(8,128)S(1)}, u32[]{:S(2)}, u32[]{:S(2)}) collective-permute-start(f32[320,128]{1,0:T(8,128)S(1)} %get-tuple-element.45), channel_id=1, source_target_pairs={{0,4},{1,129},{2,130},{3,7},{4,0},{5,133},{6,134},{7,3},{8,136},{9... | collective-permute-start | bytes 491528 | tf_op jit(solution)/shard_map/ppermute | solution.py:67
  36.4 6.2 %collective-permute-start.6 = (f32[320,128]{1,0:T(8,128)S(1)}, f32[320,128]{1,0:T(8,128)S(1)}, u32[]{:S(2)}, u32[]{:S(2)}) collective-permute-start(f32[320,128]{1,0:T(8,128)S(1)} %get-tuple-element.46), channel_id=1, source_target_pairs={{0,3},{1,64},{2,67},{3,4},{4,7},{5,68},{6,71},{7,0},{8,73},{9,10},... | collective-permute-start | bytes 491528 | tf_op jit(solution)/shard_map/ppermute | solution.py:67
  37.1 5.6 %collective-permute-start.7 = (f32[320,128]{1,0:T(8,128)S(1)}, f32[320,128]{1,0:T(8,128)S(1)}, u32[]{:S(2)}, u32[]{:S(2)}) collective-permute-start(f32[320,128]{1,0:T(8,128)S(1)} %get-tuple-element.47), channel_id=1, source_target_pairs={{0,7},{1,192},{2,195},{3,0},{4,3},{5,196},{6,199},{7,4},{8,201},{9... | collective-permute-start | bytes 491528 | tf_op jit(solution)/shard_map/ppermute | solution.py:67
  42.7 4.6 %collective-permute-start.9 = (f32[160,128]{1,0:T(8,128)S(1)}, f32[160,128]{1,0:T(8,128)S(1)}, u32[]{:S(2)}, u32[]{:S(2)}) collective-permute-start(f32[160,128]{1,0:T(8,128)S(1)} %slice_select_fusion), channel_id=1, source_target_pairs={{0,9},{1,8},{2,11},{3,10},{4,13},{5,12},{6,15},{7,14},{8,1},{9,0},... | collective-permute-start | bytes 245768 | tf_op jit(solution)/shard_map/ppermute | solution.py:55
  47.3 9.2 %collective-permute-start.12 = (f32[160,128]{1,0:T(8,128)S(1)}, f32[160,128]{1,0:T(8,128)S(1)}, u32[]{:S(2)}, u32[]{:S(2)}) collective-permute-start(f32[160,128]{1,0:T(8,128)S(1)} %select_add_fusion), channel_id=1, source_target_pairs={{0,32},{1,33},{2,34},{3,35},{4,36},{5,37},{6,38},{7,39},{8,40},{9,... | collective-permute-start | bytes 245768 | tf_op jit(solution)/shard_map/ppermute | solution.py:55
  54.0 8.0 %collective-permute-start.11 = (f32[160,128]{1,0:T(8,128)S(1)}, f32[160,128]{1,0:T(8,128)S(1)}, u32[]{:S(2)}, u32[]{:S(2)}) collective-permute-start(f32[160,128]{1,0:T(8,128)S(1)} %select_add_fusion), channel_id=1, source_target_pairs={{0,57},{1,56},{2,59},{3,58},{4,61},{5,60},{6,63},{7,62},{8,49},{9,... | collective-permute-start | bytes 245768 | tf_op jit(solution)/shard_map/ppermute | solution.py:55
  54.0 8.0 %collective-permute-start.10 = (f32[160,128]{1,0:T(8,128)S(1)}, f32[160,128]{1,0:T(8,128)S(1)}, u32[]{:S(2)}, u32[]{:S(2)}) collective-permute-start(f32[160,128]{1,0:T(8,128)S(1)} %select_add_fusion), channel_id=1, source_target_pairs={{0,25},{1,24},{2,27},{3,26},{4,29},{5,28},{6,31},{7,30},{8,17},{9,... | collective-permute-start | bytes 245768 | tf_op jit(solution)/shard_map/ppermute | solution.py:55
  62.0 4.5 %collective-permute-start.13 = (f32[160,128]{1,0:T(8,128)S(1)}, f32[160,128]{1,0:T(8,128)S(1)}, u32[]{:S(2)}, u32[]{:S(2)}) collective-permute-start(f32[160,128]{1,0:T(8,128)S(1)} %add_add_fusion), channel_id=1, source_target_pairs={{0,9},{1,8},{2,11},{3,10},{4,13},{5,12},{6,15},{7,14},{8,1},{9,0},... | collective-permute-start | bytes 245768 | tf_op jit(solution)/shard_map/ppermute | solution.py:55
  66.6 4.8 %collective-permute-start.14 = (f32[320,128]{1,0:T(8,128)S(1)}, f32[320,128]{1,0:T(8,128)S(1)}, u32[]{:S(2)}, u32[]{:S(2)}) collective-permute-start(f32[320,128]{1,0:T(8,128)S(1)} %pad_maximum_fusion.2), channel_id=1, source_target_pairs={{0,7},{1,192},{2,195},{3,0},{4,3},{5,196},{6,199},{7,4},{8,201},{9... | collective-permute-start | bytes 491528 | tf_op jit(solution)/shard_map/ppermute | solution.py:67
  68.8 7.5 %collective-permute-start.15 = (f32[320,128]{1,0:T(8,128)S(1)}, f32[320,128]{1,0:T(8,128)S(1)}, u32[]{:S(2)}, u32[]{:S(2)}) collective-permute-start(f32[320,128]{1,0:T(8,128)S(1)} %pad_maximum_fusion.2), channel_id=1, source_target_pairs={{0,3},{1,64},{2,67},{3,4},{4,7},{5,68},{6,71},{7,0},{8,73},{9,10},... | collective-permute-start | bytes 491528 | tf_op jit(solution)/shard_map/ppermute | solution.py:67
  68.8 7.5 %collective-permute-start.16 = (f32[320,128]{1,0:T(8,128)S(1)}, f32[320,128]{1,0:T(8,128)S(1)}, u32[]{:S(2)}, u32[]{:S(2)}) collective-permute-start(f32[320,128]{1,0:T(8,128)S(1)} %pad_maximum_fusion.2), channel_id=1, source_target_pairs={{0,4},{1,129},{2,130},{3,7},{4,0},{5,133},{6,134},{7,3},{8,136},{9... | collective-permute-start | bytes 491528 | tf_op jit(solution)/shard_map/ppermute | solution.py:67
  76.4 8.0 %collective-permute-start.19 = (f32[2,320,128]{2,1,0:T(8,128)S(1)}, f32[2,320,128]{2,1,0:T(8,128)S(1)}, u32[]{:S(2)}, u32[]{:S(2)}) collective-permute-start(f32[2,320,128]{2,1,0:T(8,128)S(1)} %get-tuple-element.43), channel_id=1, source_target_pairs={{0,193},{1,6},{2,5},{3,194},{4,197},{5,2},{6,1},{7,198},{8,15},{9,... | collective-permute-start | bytes 983048 | tf_op jit(solution)/shard_map/ppermute | solution.py:55
  79.6 6.5 %collective-permute-start.17 = (f32[2,320,128]{2,1,0:T(8,128)S(1)}, f32[2,320,128]{2,1,0:T(8,128)S(1)}, u32[]{:S(2)}, u32[]{:S(2)}) collective-permute-start(f32[2,320,128]{2,1,0:T(8,128)S(1)} %get-tuple-element.44), channel_id=1, source_target_pairs={{0,65},{1,2},{2,1},{3,66},{4,69},{5,6},{6,5},{7,70},{8,11},{9,72},... | collective-permute-start | bytes 983048 | tf_op jit(solution)/shard_map/ppermute | solution.py:55
  84.4 10.4 %collective-permute-start.20 = (f32[4,320,128]{2,1,0:T(8,128)S(1)}, f32[4,320,128]{2,1,0:T(8,128)S(1)}, u32[]{:S(2)}, u32[]{:S(2)}) collective-permute-start(f32[4,320,128]{2,1,0:T(8,128)S(1)} %pad_maximum_fusion.1.piece), channel_id=1, source_target_pairs={{0,65},{1,2},{2,1},{3,66},{4,69},{5,6},{6,5},{7,70},{8,11},{9,72},... | collective-permute-start | bytes 1966088 | tf_op jit(solution)/shard_map/ppermute | solution.py:55
  86.2 11.3 %collective-permute-start.18 = (f32[4,320,128]{2,1,0:T(8,128)S(1)}, f32[4,320,128]{2,1,0:T(8,128)S(1)}, u32[]{:S(2)}, u32[]{:S(2)}) collective-permute-start(f32[4,320,128]{2,1,0:T(8,128)S(1)} %pad_maximum_fusion.piece), channel_id=1, source_target_pairs={{0,193},{1,6},{2,5},{3,194},{4,197},{5,2},{6,1},{7,198},{8,15},{9,... | collective-permute-start | bytes 1966088 | tf_op jit(solution)/shard_map/ppermute | solution.py:55
  99.1 16.8 %collective-permute-start.23 = (bf16[960,512]{1,0:T(8,128)(2,1)S(1)}, bf16[960,512]{1,0:T(8,128)(2,1)S(1)}, u32[]{:S(2)}, u32[]{:S(2)}) collective-permute-start(bf16[960,512]{1,0:T(8,128)(2,1)S(1)} %get-tuple-element.36.refs_1_), channel_id=1, source_target_pairs={{0,1},{1,0},{2,3},{3,2},{4,5},{5,4},{6,7},{7,6},{8,9},{9,8},{10,11... | collective-permute-start | bytes 2949128 | tf_op jit(solution)/shard_map/ppermute | solution.py:42
  99.4 16.5 %collective-permute-start.22 = (bf16[960,512]{1,0:T(8,128)(2,1)S(1)}, bf16[960,512]{1,0:T(8,128)(2,1)S(1)}, u32[]{:S(2)}, u32[]{:S(2)}) collective-permute-start(bf16[960,512]{1,0:T(8,128)(2,1)S(1)} %get-tuple-element.35.refs_0_), channel_id=1, source_target_pairs={{0,1},{1,0},{2,3},{3,2},{4,5},{5,4},{6,7},{7,6},{8,9},{9,8},{10,11... | collective-permute-start | bytes 2949128 | tf_op jit(solution)/shard_map/ppermute | solution.py:42
  99.6 16.3 %collective-permute-start.25 = (bf16[960,512]{1,0:T(8,128)(2,1)S(1)}, bf16[960,512]{1,0:T(8,128)(2,1)S(1)}, u32[]{:S(2)}, u32[]{:S(2)}) collective-permute-start(bf16[960,512]{1,0:T(8,128)(2,1)S(1)} %get-tuple-element.38.refs_3_), channel_id=1, source_target_pairs={{0,1},{1,0},{2,3},{3,2},{4,5},{5,4},{6,7},{7,6},{8,9},{9,8},{10,11... | collective-permute-start | bytes 2949128 | tf_op jit(solution)/shard_map/ppermute | solution.py:42
  99.9 16.0 %collective-permute-start.24 = (bf16[960,512]{1,0:T(8,128)(2,1)S(1)}, bf16[960,512]{1,0:T(8,128)(2,1)S(1)}, u32[]{:S(2)}, u32[]{:S(2)}) collective-permute-start(bf16[960,512]{1,0:T(8,128)(2,1)S(1)} %get-tuple-element.37.refs_2_), channel_id=1, source_target_pairs={{0,1},{1,0},{2,3},{3,2},{4,5},{5,4},{6,7},{7,6},{8,9},{9,8},{10,11... | collective-permute-start | bytes 2949128 | tf_op jit(solution)/shard_map/ppermute | solution.py:42
  (5 other events, 40.6 us)
